TPU v7x, 32 devices: a whole 2x2x4 slice. The times are simulated.
32 devices in a mesh: groups: 2 (over y), rows: 8 (over z, x), cols: 2 (over core).
Axes of the slice: x: 2, y: 2, z: 4, core: 2. Of those that a mesh axis runs over, the one named last changes fastest.
Arguments:
- features: bfloat16 [64, 4096], P(('groups', 'rows'), 'cols'), parts along dimension 0, may hold values from -6 to 6
- weights: bfloat16 [4, 2, 8, 6, 256, 256], P(None, 'cols', 'rows'), may hold values from -0.25 to 0.25
- active: int32 [4, 2, 8, 6], P(None, 'cols', 'rows'), may hold values 0 or 1
- layer_bias: float32 [4, 2, 8, 256], P(None, 'cols', 'rows'), may hold values from -0.5 to 0.3
Outputs:
- activations: bfloat16 [64, 4096], P(('groups', 'rows'), 'cols'), parts along dimension 0
There are 2 independent parts, one for each index of `groups`. A program takes and returns all parts, laid end to end along the dimension named above; an argument that names none is the same for every part. Nothing has to cross between parts.
Inputs may be any that keep to these rules, and one draw needn't show every extreme that they name: `active`: 1 marks a source block that feeds the output block.
All inputs are finite; a program needn't handle non-finite values.
Results may differ from a plain program's by a relative error of at most 0.0066.
Values may be sent and summed in bfloat16 or wider, within the bound.
No kernel may reach another device: no remote copies, remote signals or barrier semaphores. Data moves between devices by JAX's collectives and lax.ppermute only.
A program may use at most 64 MiB of HBM per device.

v0:
```python
import jax
import jax.numpy as jnp
from jax import lax
from jax.sharding import PartitionSpec as P


def from_behind(block, axis, distance):
    devices = range(lax.axis_size(axis))
    route = [((i - distance) % len(devices), i) for i in devices]
    return lax.ppermute(block, axis, route)


def from_partner(value, axis, apart):
    mask = 2**apart
    pairs = [(source, source ^ mask) for source in range(lax.axis_size(axis))]
    return lax.ppermute(value, axis, pairs)


def neuron_layer(current_activation, weight_set, active_set, bias_row):
    reach_blocks = (weight_set.shape[0] - 2) // 2
    gathered = []
    for source_position in range(2 * reach_blocks + 1):
        offset = reach_blocks - source_position
        if offset == 0:
            gathered.append(current_activation)
        else:
            gathered.append(from_behind(current_activation, "rows", offset))
    partner = from_partner(current_activation, "cols", 0)
    gathered.append(partner)
    source_blocks = jnp.stack(gathered, axis=0)
    masked_output = jnp.where(active_set[:, None, None] > 0, weight_set, jnp.zeros_like(weight_set))
    running_sum = jnp.einsum(
        "nqf,nfg->qg", source_blocks, masked_output, preferred_element_type=jnp.float32
    )
    return jnp.maximum(running_sum + bias_row[None, :], 0.0).astype(jnp.bfloat16)


def on_device(features, weights, active, layer_bias):
    layer_count = weights.shape[0]
    current_activation = features
    for layer_position in range(layer_count):
        spread = lax.all_to_all(current_activation, "rows", split_axis=1, concat_axis=0, tiled=True)
        spread = neuron_layer(
            spread,
            weights[layer_position, 0, 0],
            active[layer_position, 0, 0],
            layer_bias[layer_position, 0, 0],
        )
        current_activation = lax.all_to_all(spread, "rows", split_axis=0, concat_axis=1, tiled=True)
    return current_activation


def solution(mesh):
    in_specs = (
        P(("groups", "rows"), "cols"),
        P(None, "cols", "rows", None, None, None),
        P(None, "cols", "rows", None),
        P(None, "cols", "rows", None),
    )
    out_specs = P(("groups", "rows"), "cols")
    return jax.shard_map(
        on_device, mesh=mesh, in_specs=in_specs, out_specs=out_specs, check_vma=False
    )
```

profile of v0, /device:TPU:0, one launch (start us, length us, event | category | flops | bytes accessed | tf_op | source)
XLA Modules:
  0.0 126.2 jit_solution(13561283612043357516)
XLA Ops:
  0.0 0.0 copy-start
  0.0 7.5 %all-to-all-start = ((bf16[4,8,256]{2,0,1:T(4,128)(2,1)}), bf16[4,8,256]{2,0,1:T(4,128)(2,1)S(1)}, u32[]{:S(2)}, u32[]{:S(2)}) async-start(bf16[4,8,256]{2,0,1:T(4,128)(2,1)} %bitcast.123), calls=%async_computation | async-start | bytes 32768 | tf_op jit(solution)/shard_map/all_to_all | solution.py:42
  7.5 0.7 fusion.28
  8.2 5.8 %all-to-all-done = bf16[4,8,256]{2,0,1:T(4,128)(2,1)S(1)} async-done(((bf16[4,8,256]{2,0,1:T(4,128)(2,1)}), bf16[4,8,256]{2,0,1:T(4,128)(2,1)S(1)}, u32[]{:S(2)}, u32[]{:S(2)}) %all-to-all-start) | async-done | bytes 16416 | tf_op jit(solution)/shard_map/all_to_all | solution.py:42
  14.1 0.5 collective-permute-start
  14.6 0.7 compare_bitcast_fusion
  15.3 0.7 collective-permute-start.1
  16.0 4.1 %collective-permute-start.2 = (bf16[32,256]{1,0:T(8,128)(2,1)S(1)}, bf16[32,256]{1,0:T(8,128)(2,1)S(1)}, u32[]{:S(2)}, u32[]{:S(2)}) collective-permute-start(bf16[32,256]{1,0:T(8,128)(2,1)S(1)} %all_to_all.103), channel_id=1, source_target_pairs={{2,0},{4,2},{6,4},{8,6},{10,8},{12,10},{14,12},{0,14},{3,1},{5,3},... | collective-permute-start | bytes 49160 | tf_op jit(solution)/shard_map/ppermute | solution.py:10
  20.1 1.6 %collective-permute-start.3 = (bf16[32,256]{1,0:T(8,128)(2,1)S(1)}, bf16[32,256]{1,0:T(8,128)(2,1)S(1)}, u32[]{:S(2)}, u32[]{:S(2)}) collective-permute-start(bf16[32,256]{1,0:T(8,128)(2,1)S(1)} %all_to_all.103), channel_id=1, source_target_pairs={{4,0},{6,2},{8,4},{10,6},{12,8},{14,10},{0,12},{2,14},{5,1},{7,3},... | collective-permute-start | bytes 49160 | tf_op jit(solution)/shard_map/ppermute | solution.py:10
  21.7 0.0 collective-permute-start.4
  21.7 0.0 collective-permute-done
  21.7 0.1 collective-permute-done.1
  21.8 0.0 collective-permute-done.2
  21.8 2.1 %collective-permute-done.3 = bf16[32,256]{1,0:T(8,128)(2,1)S(1)} collective-permute-done((bf16[32,256]{1,0:T(8,128)(2,1)S(1)}, bf16[32,256]{1,0:T(8,128)(2,1)S(1)}, u32[]{:S(2)}, u32[]{:S(2)}) %collective-permute-start.3) | collective-permute-done | bytes 16416 | tf_op jit(solution)/shard_map/ppermute | solution.py:10
  23.9 0.0 collective-permute-done.4
  23.9 1.5 %fusion.8 = bf16[32,256]{1,0:T(8,128)(2,1)S(1)} fusion(bf16[6,32,256]{2,1,0:T(8,128)(2,1)S(1)} %constant_dynamic-update-slice_fusion, bf16[4,1,1,6,256,256]{5,4,3,2,1,0:T(8,128)(2,1)} %param.5, pred[6]{0:T(512)(128)(4,1)S(1)} %get-tuple-element.11, f32[256]{0:T(256)S(1)} %bitcast.127), kind=kOutput, calls=%fused_computation.12 | convolution fusion | flops 25583616 | bytes 902150 | tf_op jit(solution)/shard_map/nqf,nfg->qg/dot_general | solution.py:32
  25.4 11.0 %all_to_all.134 = bf16[8,4,256]{2,1,0:T(4,128)(2,1)S(1)} all-to-all(bf16[8,4,256]{2,1,0:T(4,128)(2,1)S(1)} %all_to_all.104), channel_id=1, replica_groups=mesh['groups'=2,'rows'=8,'cols'=2] {'rows'}, dimensions={0} | all-to-all | bytes 32768 | tf_op jit(solution)/shard_map/all_to_all | solution.py:49
  36.4 8.9 %all_to_all.135 = bf16[4,8,256]{2,0,1:T(4,128)(2,1)S(1)} all-to-all(bf16[4,8,256]{2,0,1:T(4,128)(2,1)S(1)} %bitcast.119), channel_id=1, replica_groups=mesh['groups'=2,'rows'=8,'cols'=2] {'rows'}, dimensions={1} | all-to-all | bytes 32768 | tf_op jit(solution)/shard_map/all_to_all | solution.py:42
  45.3 0.5 collective-permute-start.5
  45.8 0.7 collective-permute-start.6
  46.6 4.0 %collective-permute-start.7 = (bf16[32,256]{1,0:T(8,128)(2,1)S(1)}, bf16[32,256]{1,0:T(8,128)(2,1)S(1)}, u32[]{:S(2)}, u32[]{:S(2)}) collective-permute-start(bf16[32,256]{1,0:T(8,128)(2,1)S(1)} %all_to_all.109), channel_id=1, source_target_pairs={{2,0},{4,2},{6,4},{8,6},{10,8},{12,10},{14,12},{0,14},{3,1},{5,3},... | collective-permute-start | bytes 49160 | tf_op jit(solution)/shard_map/ppermute | solution.py:10
  50.6 1.6 %collective-permute-start.8 = (bf16[32,256]{1,0:T(8,128)(2,1)S(1)}, bf16[32,256]{1,0:T(8,128)(2,1)S(1)}, u32[]{:S(2)}, u32[]{:S(2)}) collective-permute-start(bf16[32,256]{1,0:T(8,128)(2,1)S(1)} %all_to_all.109), channel_id=1, source_target_pairs={{4,0},{6,2},{8,4},{10,6},{12,8},{14,10},{0,12},{2,14},{5,1},{7,3},... | collective-permute-start | bytes 49160 | tf_op jit(solution)/shard_map/ppermute | solution.py:10
  52.2 0.0 collective-permute-start.9
  52.2 0.0 collective-permute-done.5
  52.2 0.1 collective-permute-done.6
  52.3 0.0 collective-permute-done.7
  52.3 2.1 %collective-permute-done.8 = bf16[32,256]{1,0:T(8,128)(2,1)S(1)} collective-permute-done((bf16[32,256]{1,0:T(8,128)(2,1)S(1)}, bf16[32,256]{1,0:T(8,128)(2,1)S(1)}, u32[]{:S(2)}, u32[]{:S(2)}) %collective-permute-start.8) | collective-permute-done | bytes 16416 | tf_op jit(solution)/shard_map/ppermute | solution.py:10
  54.4 0.0 collective-permute-done.9
  54.4 1.5 %fusion.9 = bf16[32,256]{1,0:T(8,128)(2,1)S(1)} fusion(bf16[6,32,256]{2,1,0:T(8,128)(2,1)S(1)} %constant_dynamic-update-slice_fusion.6, bf16[4,1,1,6,256,256]{5,4,3,2,1,0:T(8,128)(2,1)} %param.5, pred[6]{0:T(512)(128)(4,1)S(1)} %get-tuple-element.10, f32[256]{0:T(256)S(1)} %bitcast.126), kind=kOutput, calls=%fused_computation.13 | convolution fusion | flops 25583616 | bytes 902150 | tf_op jit(solution)/shard_map/nqf,nfg->qg/dot_general | solution.py:32
  55.8 11.0 %all_to_all.136 = bf16[8,4,256]{2,1,0:T(4,128)(2,1)S(1)} all-to-all(bf16[8,4,256]{2,1,0:T(4,128)(2,1)S(1)} %all_to_all.110), channel_id=1, replica_groups=mesh['groups'=2,'rows'=8,'cols'=2] {'rows'}, dimensions={0} | all-to-all | bytes 32768 | tf_op jit(solution)/shard_map/all_to_all | solution.py:49
  66.8 8.9 %all_to_all.137 = bf16[4,8,256]{2,0,1:T(4,128)(2,1)S(1)} all-to-all(bf16[4,8,256]{2,0,1:T(4,128)(2,1)S(1)} %bitcast.120), channel_id=1, replica_groups=mesh['groups'=2,'rows'=8,'cols'=2] {'rows'}, dimensions={1} | all-to-all | bytes 32768 | tf_op jit(solution)/shard_map/all_to_all | solution.py:42
  75.8 0.5 collective-permute-start.10
  76.3 0.7 collective-permute-start.11
  77.1 4.0 %collective-permute-start.12 = (bf16[32,256]{1,0:T(8,128)(2,1)S(1)}, bf16[32,256]{1,0:T(8,128)(2,1)S(1)}, u32[]{:S(2)}, u32[]{:S(2)}) collective-permute-start(bf16[32,256]{1,0:T(8,128)(2,1)S(1)} %all_to_all.115), channel_id=1, source_target_pairs={{2,0},{4,2},{6,4},{8,6},{10,8},{12,10},{14,12},{0,14},{3,1},{5,3},... | collective-permute-start | bytes 49160 | tf_op jit(solution)/shard_map/ppermute | solution.py:10
  81.1 1.6 %collective-permute-start.13 = (bf16[32,256]{1,0:T(8,128)(2,1)S(1)}, bf16[32,256]{1,0:T(8,128)(2,1)S(1)}, u32[]{:S(2)}, u32[]{:S(2)}) collective-permute-start(bf16[32,256]{1,0:T(8,128)(2,1)S(1)} %all_to_all.115), channel_id=1, source_target_pairs={{4,0},{6,2},{8,4},{10,6},{12,8},{14,10},{0,12},{2,14},{5,1},{7,3},... | collective-permute-start | bytes 49160 | tf_op jit(solution)/shard_map/ppermute | solution.py:10
  82.6 0.0 collective-permute-start.14
  82.7 0.0 collective-permute-done.10
  82.7 0.1 collective-permute-done.11
  82.8 0.0 collective-permute-done.12
  82.8 2.1 %collective-permute-done.13 = bf16[32,256]{1,0:T(8,128)(2,1)S(1)} collective-permute-done((bf16[32,256]{1,0:T(8,128)(2,1)S(1)}, bf16[32,256]{1,0:T(8,128)(2,1)S(1)}, u32[]{:S(2)}, u32[]{:S(2)}) %collective-permute-start.13) | collective-permute-done | bytes 16416 | tf_op jit(solution)/shard_map/ppermute | solution.py:10
  84.8 0.0 collective-permute-done.14
  84.8 0.0 copy-done
  84.9 0.3 fusion.10
  85.2 11.0 %all_to_all.138 = bf16[8,4,256]{2,1,0:T(4,128)(2,1)S(1)} all-to-all(bf16[8,4,256]{2,1,0:T(4,128)(2,1)S(1)} %all_to_all.116), channel_id=1, replica_groups=mesh['groups'=2,'rows'=8,'cols'=2] {'rows'}, dimensions={0} | all-to-all | bytes 32768 | tf_op jit(solution)/shard_map/all_to_all | solution.py:49
  96.2 8.9 %all_to_all.139 = bf16[4,8,256]{2,0,1:T(4,128)(2,1)S(1)} all-to-all(bf16[4,8,256]{2,0,1:T(4,128)(2,1)S(1)} %bitcast.121), channel_id=1, replica_groups=mesh['groups'=2,'rows'=8,'cols'=2] {'rows'}, dimensions={1} | all-to-all | bytes 32768 | tf_op jit(solution)/shard_map/all_to_all | solution.py:42
  105.1 0.5 collective-permute-start.15
  105.7 0.7 collective-permute-start.16
  106.4 4.0 %collective-permute-start.17 = (bf16[32,256]{1,0:T(8,128)(2,1)S(1)}, bf16[32,256]{1,0:T(8,128)(2,1)S(1)}, u32[]{:S(2)}, u32[]{:S(2)}) collective-permute-start(bf16[32,256]{1,0:T(8,128)(2,1)S(1)} %all_to_all.121), channel_id=1, source_target_pairs={{2,0},{4,2},{6,4},{8,6},{10,8},{12,10},{14,12},{0,14},{3,1},{5,3},... | collective-permute-start | bytes 49160 | tf_op jit(solution)/shard_map/ppermute | solution.py:10
  110.5 1.6 %collective-permute-start.18 = (bf16[32,256]{1,0:T(8,128)(2,1)S(1)}, bf16[32,256]{1,0:T(8,128)(2,1)S(1)}, u32[]{:S(2)}, u32[]{:S(2)}) collective-permute-start(bf16[32,256]{1,0:T(8,128)(2,1)S(1)} %all_to_all.121), channel_id=1, source_target_pairs={{4,0},{6,2},{8,4},{10,6},{12,8},{14,10},{0,12},{2,14},{5,1},{7,3},... | collective-permute-start | bytes 49160 | tf_op jit(solution)/shard_map/ppermute | solution.py:10
  112.0 0.0 collective-permute-start.19
  112.0 0.0 collective-permute-done.15
  112.0 0.1 collective-permute-done.16
  112.1 0.0 collective-permute-done.17
  112.1 2.1 %collective-permute-done.18 = bf16[32,256]{1,0:T(8,128)(2,1)S(1)} collective-permute-done((bf16[32,256]{1,0:T(8,128)(2,1)S(1)}, bf16[32,256]{1,0:T(8,128)(2,1)S(1)}, u32[]{:S(2)}, u32[]{:S(2)}) %collective-permute-start.18) | collective-permute-done | bytes 16416 | tf_op jit(solution)/shard_map/ppermute | solution.py:10
  114.2 0.0 collective-permute-done.19
  114.2 0.3 fusion.11
  114.6 11.0 %all_to_all.140 = bf16[8,4,256]{2,1,0:T(4,128)(2,1)S(1)} all-to-all(bf16[8,4,256]{2,1,0:T(4,128)(2,1)S(1)} %all_to_all.122), channel_id=1, replica_groups=mesh['groups'=2,'rows'=8,'cols'=2] {'rows'}, dimensions={0} | all-to-all | bytes 32768 | tf_op jit(solution)/shard_map/all_to_all | solution.py:49
  125.5 0.6 copy.28
  (36 shorter events, 0.2 us)
Async XLA Ops:
  0.0 84.9 %copy-start = (bf16[4,1,1,6,256,256]{5,4,3,2,1,0:T(8,128)(2,1)S(1)}, bf16[4,1,1,6,256,256]{5,4,3,2,1,0:T(8,128)(2,1)}, u32[]{:S(2)}) copy-start(bf16[4,1,1,6,256,256]{5,4,3,2,1,0:T(8,128)(2,1)} %param.5) | copy-start | bytes 9437188
  0.0 14.1 %all-to-all-start = ((bf16[4,8,256]{2,0,1:T(4,128)(2,1)}), bf16[4,8,256]{2,0,1:T(4,128)(2,1)S(1)}, u32[]{:S(2)}, u32[]{:S(2)}) async-start(bf16[4,8,256]{2,0,1:T(4,128)(2,1)} %bitcast.123), calls=%async_computation | async-start | bytes 32768 | tf_op jit(solution)/shard_map/all_to_all | solution.py:42
  14.1 7.6 %collective-permute-start = (bf16[32,256]{1,0:T(8,128)(2,1)S(1)}, bf16[32,256]{1,0:T(8,128)(2,1)S(1)}, u32[]{:S(2)}, u32[]{:S(2)}) collective-permute-start(bf16[32,256]{1,0:T(8,128)(2,1)S(1)} %all_to_all.103), channel_id=1, source_target_pairs={{12,0},{14,2},{0,4},{2,6},{4,8},{6,10},{8,12},{10,14},{13,1},{15,3... | collective-permute-start | bytes 49160 | tf_op jit(solution)/shard_map/ppermute | solution.py:10
  15.3 6.4 %collective-permute-start.1 = (bf16[32,256]{1,0:T(8,128)(2,1)S(1)}, bf16[32,256]{1,0:T(8,128)(2,1)S(1)}, u32[]{:S(2)}, u32[]{:S(2)}) collective-permute-start(bf16[32,256]{1,0:T(8,128)(2,1)S(1)} %all_to_all.103), channel_id=1, source_target_pairs={{14,0},{0,2},{2,4},{4,6},{6,8},{8,10},{10,12},{12,14},{15,1},{1,3}... | collective-permute-start | bytes 49160 | tf_op jit(solution)/shard_map/ppermute | solution.py:10
  16.0 5.8 %collective-permute-start.2 = (bf16[32,256]{1,0:T(8,128)(2,1)S(1)}, bf16[32,256]{1,0:T(8,128)(2,1)S(1)}, u32[]{:S(2)}, u32[]{:S(2)}) collective-permute-start(bf16[32,256]{1,0:T(8,128)(2,1)S(1)} %all_to_all.103), channel_id=1, source_target_pairs={{2,0},{4,2},{6,4},{8,6},{10,8},{12,10},{14,12},{0,14},{3,1},{5,3},... | collective-permute-start | bytes 49160 | tf_op jit(solution)/shard_map/ppermute | solution.py:10
  20.1 3.7 %collective-permute-start.3 = (bf16[32,256]{1,0:T(8,128)(2,1)S(1)}, bf16[32,256]{1,0:T(8,128)(2,1)S(1)}, u32[]{:S(2)}, u32[]{:S(2)}) collective-permute-start(bf16[32,256]{1,0:T(8,128)(2,1)S(1)} %all_to_all.103), channel_id=1, source_target_pairs={{4,0},{6,2},{8,4},{10,6},{12,8},{14,10},{0,12},{2,14},{5,1},{7,3},... | collective-permute-start | bytes 49160 | tf_op jit(solution)/shard_map/ppermute | solution.py:10
  21.7 2.2 %collective-permute-start.4 = (bf16[32,256]{1,0:T(8,128)(2,1)S(1)}, bf16[32,256]{1,0:T(8,128)(2,1)S(1)}, u32[]{:S(2)}, u32[]{:S(2)}) collective-permute-start(bf16[32,256]{1,0:T(8,128)(2,1)S(1)} %all_to_all.103), channel_id=1, source_target_pairs={{0,1},{1,0},{2,3},{3,2},{4,5},{5,4},{6,7},{7,6},{8,9},{9,8},{10,11... | collective-permute-start | bytes 49160 | tf_op jit(solution)/shard_map/ppermute | solution.py:16
  45.3 6.9 %collective-permute-start.5 = (bf16[32,256]{1,0:T(8,128)(2,1)S(1)}, bf16[32,256]{1,0:T(8,128)(2,1)S(1)}, u32[]{:S(2)}, u32[]{:S(2)}) collective-permute-start(bf16[32,256]{1,0:T(8,128)(2,1)S(1)} %all_to_all.109), channel_id=1, source_target_pairs={{12,0},{14,2},{0,4},{2,6},{4,8},{6,10},{8,12},{10,14},{13,1},{15,3... | collective-permute-start | bytes 49160 | tf_op jit(solution)/shard_map/ppermute | solution.py:10
  45.8 6.4 %collective-permute-start.6 = (bf16[32,256]{1,0:T(8,128)(2,1)S(1)}, bf16[32,256]{1,0:T(8,128)(2,1)S(1)}, u32[]{:S(2)}, u32[]{:S(2)}) collective-permute-start(bf16[32,256]{1,0:T(8,128)(2,1)S(1)} %all_to_all.109), channel_id=1, source_target_pairs={{14,0},{0,2},{2,4},{4,6},{6,8},{8,10},{10,12},{12,14},{15,1},{1,3}... | collective-permute-start | bytes 49160 | tf_op jit(solution)/shard_map/ppermute | solution.py:10
  46.6 5.7 %collective-permute-start.7 = (bf16[32,256]{1,0:T(8,128)(2,1)S(1)}, bf16[32,256]{1,0:T(8,128)(2,1)S(1)}, u32[]{:S(2)}, u32[]{:S(2)}) collective-permute-start(bf16[32,256]{1,0:T(8,128)(2,1)S(1)} %all_to_all.109), channel_id=1, source_target_pairs={{2,0},{4,2},{6,4},{8,6},{10,8},{12,10},{14,12},{0,14},{3,1},{5,3},... | collective-permute-start | bytes 49160 | tf_op jit(solution)/shard_map/ppermute | solution.py:10
  50.6 3.7 %collective-permute-start.8 = (bf16[32,256]{1,0:T(8,128)(2,1)S(1)}, bf16[32,256]{1,0:T(8,128)(2,1)S(1)}, u32[]{:S(2)}, u32[]{:S(2)}) collective-permute-start(bf16[32,256]{1,0:T(8,128)(2,1)S(1)} %all_to_all.109), channel_id=1, source_target_pairs={{4,0},{6,2},{8,4},{10,6},{12,8},{14,10},{0,12},{2,14},{5,1},{7,3},... | collective-permute-start | bytes 49160 | tf_op jit(solution)/shard_map/ppermute | solution.py:10
  52.2 2.2 %collective-permute-start.9 = (bf16[32,256]{1,0:T(8,128)(2,1)S(1)}, bf16[32,256]{1,0:T(8,128)(2,1)S(1)}, u32[]{:S(2)}, u32[]{:S(2)}) collective-permute-start(bf16[32,256]{1,0:T(8,128)(2,1)S(1)} %all_to_all.109), channel_id=1, source_target_pairs={{0,1},{1,0},{2,3},{3,2},{4,5},{5,4},{6,7},{7,6},{8,9},{9,8},{10,11... | collective-permute-start | bytes 49160 | tf_op jit(solution)/shard_map/ppermute | solution.py:16
  75.8 6.9 %collective-permute-start.10 = (bf16[32,256]{1,0:T(8,128)(2,1)S(1)}, bf16[32,256]{1,0:T(8,128)(2,1)S(1)}, u32[]{:S(2)}, u32[]{:S(2)}) collective-permute-start(bf16[32,256]{1,0:T(8,128)(2,1)S(1)} %all_to_all.115), channel_id=1, source_target_pairs={{12,0},{14,2},{0,4},{2,6},{4,8},{6,10},{8,12},{10,14},{13,1},{15,3... | collective-permute-start | bytes 49160 | tf_op jit(solution)/shard_map/ppermute | solution.py:10
  76.3 6.4 %collective-permute-start.11 = (bf16[32,256]{1,0:T(8,128)(2,1)S(1)}, bf16[32,256]{1,0:T(8,128)(2,1)S(1)}, u32[]{:S(2)}, u32[]{:S(2)}) collective-permute-start(bf16[32,256]{1,0:T(8,128)(2,1)S(1)} %all_to_all.115), channel_id=1, source_target_pairs={{14,0},{0,2},{2,4},{4,6},{6,8},{8,10},{10,12},{12,14},{15,1},{1,3}... | collective-permute-start | bytes 49160 | tf_op jit(solution)/shard_map/ppermute | solution.py:10
  77.1 5.7 %collective-permute-start.12 = (bf16[32,256]{1,0:T(8,128)(2,1)S(1)}, bf16[32,256]{1,0:T(8,128)(2,1)S(1)}, u32[]{:S(2)}, u32[]{:S(2)}) collective-permute-start(bf16[32,256]{1,0:T(8,128)(2,1)S(1)} %all_to_all.115), channel_id=1, source_target_pairs={{2,0},{4,2},{6,4},{8,6},{10,8},{12,10},{14,12},{0,14},{3,1},{5,3},... | collective-permute-start | bytes 49160 | tf_op jit(solution)/shard_map/ppermute | solution.py:10
  81.1 3.7 %collective-permute-start.13 = (bf16[32,256]{1,0:T(8,128)(2,1)S(1)}, bf16[32,256]{1,0:T(8,128)(2,1)S(1)}, u32[]{:S(2)}, u32[]{:S(2)}) collective-permute-start(bf16[32,256]{1,0:T(8,128)(2,1)S(1)} %all_to_all.115), channel_id=1, source_target_pairs={{4,0},{6,2},{8,4},{10,6},{12,8},{14,10},{0,12},{2,14},{5,1},{7,3},... | collective-permute-start | bytes 49160 | tf_op jit(solution)/shard_map/ppermute | solution.py:10
  82.6 2.2 %collective-permute-start.14 = (bf16[32,256]{1,0:T(8,128)(2,1)S(1)}, bf16[32,256]{1,0:T(8,128)(2,1)S(1)}, u32[]{:S(2)}, u32[]{:S(2)}) collective-permute-start(bf16[32,256]{1,0:T(8,128)(2,1)S(1)} %all_to_all.115), channel_id=1, source_target_pairs={{0,1},{1,0},{2,3},{3,2},{4,5},{5,4},{6,7},{7,6},{8,9},{9,8},{10,11... | collective-permute-start | bytes 49160 | tf_op jit(solution)/shard_map/ppermute | solution.py:16
  105.1 6.9 %collective-permute-start.15 = (bf16[32,256]{1,0:T(8,128)(2,1)S(1)}, bf16[32,256]{1,0:T(8,128)(2,1)S(1)}, u32[]{:S(2)}, u32[]{:S(2)}) collective-permute-start(bf16[32,256]{1,0:T(8,128)(2,1)S(1)} %all_to_all.121), channel_id=1, source_target_pairs={{12,0},{14,2},{0,4},{2,6},{4,8},{6,10},{8,12},{10,14},{13,1},{15,3... | collective-permute-start | bytes 49160 | tf_op jit(solution)/shard_map/ppermute | solution.py:10
  105.7 6.4 %collective-permute-start.16 = (bf16[32,256]{1,0:T(8,128)(2,1)S(1)}, bf16[32,256]{1,0:T(8,128)(2,1)S(1)}, u32[]{:S(2)}, u32[]{:S(2)}) collective-permute-start(bf16[32,256]{1,0:T(8,128)(2,1)S(1)} %all_to_all.121), channel_id=1, source_target_pairs={{14,0},{0,2},{2,4},{4,6},{6,8},{8,10},{10,12},{12,14},{15,1},{1,3}... | collective-permute-start | bytes 49160 | tf_op jit(solution)/shard_map/ppermute | solution.py:10
  106.4 5.7 %collective-permute-start.17 = (bf16[32,256]{1,0:T(8,128)(2,1)S(1)}, bf16[32,256]{1,0:T(8,128)(2,1)S(1)}, u32[]{:S(2)}, u32[]{:S(2)}) collective-permute-start(bf16[32,256]{1,0:T(8,128)(2,1)S(1)} %all_to_all.121), channel_id=1, source_target_pairs={{2,0},{4,2},{6,4},{8,6},{10,8},{12,10},{14,12},{0,14},{3,1},{5,3},... | collective-permute-start | bytes 49160 | tf_op jit(solution)/shard_map/ppermute | solution.py:10
  110.5 3.7 %collective-permute-start.18 = (bf16[32,256]{1,0:T(8,128)(2,1)S(1)}, bf16[32,256]{1,0:T(8,128)(2,1)S(1)}, u32[]{:S(2)}, u32[]{:S(2)}) collective-permute-start(bf16[32,256]{1,0:T(8,128)(2,1)S(1)} %all_to_all.121), channel_id=1, source_target_pairs={{4,0},{6,2},{8,4},{10,6},{12,8},{14,10},{0,12},{2,14},{5,1},{7,3},... | collective-permute-start | bytes 49160 | tf_op jit(solution)/shard_map/ppermute | solution.py:10
  112.0 2.2 %collective-permute-start.19 = (bf16[32,256]{1,0:T(8,128)(2,1)S(1)}, bf16[32,256]{1,0:T(8,128)(2,1)S(1)}, u32[]{:S(2)}, u32[]{:S(2)}) collective-permute-start(bf16[32,256]{1,0:T(8,128)(2,1)S(1)} %all_to_all.121), channel_id=1, source_target_pairs={{0,1},{1,0},{2,3},{3,2},{4,5},{5,4},{6,7},{7,6},{8,9},{9,8},{10,11... | collective-permute-start | bytes 49160 | tf_op jit(solution)/shard_map/ppermute | solution.py:16
where the time goes:
time: 127 us; the launch traced here: 126 us
  blocking collectives  70.8 us (56%)
  starting transfers between devices  34.9 us (27%)
  waiting for transfers between devices  14.5 us (11%)
  matrix products  3.54 us (3%)
  local copies, waits for them, and re-layouts  1.53 us (1%)
    all_to_all x4, blocking collectives, on_device(): lax.all_to_all(spread, 'rows', split_axis=0, concat_axis=1, tiled=True)  44 us
    ppermute x16, starting transfers between devices, from_behind(): return lax.ppermute(block, axis, route)  27.4 us
    all_to_all x3, blocking collectives, on_device(): lax.all_to_all(current_activation, 'rows', split_axis=1, concat_axis=0, t...  26.8 us
    ppermute x16, waiting for transfers between devices, from_behind(): return lax.ppermute(block, axis, route)  8.64 us
    all_to_all x1, starting transfers between devices, on_device(): lax.all_to_all(current_activation, 'rows', split_axis=1, concat_axis=0, t...  7.52 us
    all_to_all x1, waiting for transfers between devices, on_device(): lax.all_to_all(current_activation, 'rows', split_axis=1, concat_axis=0, t...  5.85 us
    dot_general x4, matrix products, neuron_layer(): jnp.einsum('nqf,nfg->qg', source_blocks, masked_output, preferred_element...  3.54 us
  transfers between devices with their start and end apart: 21, of which 9 were waited for; matrix products, arithmetic and copies ran while one was open for 1% of the time, Pallas kernels for 0%

commit v1 on v0

v1 whole, which is shorter than its diff:
```python
import jax
import jax.numpy as jnp
from jax import lax
from jax.sharding import PartitionSpec as P


def shifted(block, axis, distance):
    size = lax.axis_size(axis)
    return lax.ppermute(block, axis, [((i + distance) % size, i) for i in range(size)])


def partner(block):
    return lax.ppermute(block, "cols", [(i, i ^ 1) for i in range(lax.axis_size("cols"))])


def neuron_layer(sources, weight_set, active_set, bias_row):
    kept = [jnp.where(active_set[m] > 0, source, jnp.zeros_like(source)) for m, source in enumerate(sources)]
    stacked = jnp.concatenate(kept, axis=1)
    total = jnp.dot(stacked, weight_set.reshape(-1, weight_set.shape[-1]), preferred_element_type=jnp.float32)
    return jnp.maximum(total + bias_row[None, :], 0.0).astype(jnp.bfloat16)


def on_device(features, weights, active, layer_bias):
    layer_count, _, _, candidates, width, _ = weights.shape
    reach = (candidates - 2) // 2
    devices = lax.axis_size("rows")
    samples = features.shape[0]

    blocks = features.reshape(samples, devices, width).transpose(1, 0, 2)
    spread = jnp.concatenate([jnp.roll(blocks, reach - m, axis=0) for m in range(2 * reach + 1)], axis=2)
    spread = lax.all_to_all(spread, "rows", split_axis=0, concat_axis=0, tiled=True)
    spread = spread.reshape(devices * samples, (2 * reach + 1) * width)
    sources = [spread[:, m * width : (m + 1) * width] for m in range(2 * reach + 1)]
    sources.append(partner(sources[reach]))
    for layer in range(layer_count):
        if layer:
            sources = [block if m == reach else shifted(block, "rows", m - reach) for m in range(2 * reach + 1)]
            sources.append(partner(block))
        block = neuron_layer(sources, weights[layer, 0, 0], active[layer, 0, 0], layer_bias[layer, 0, 0])
    return lax.all_to_all(block, "rows", split_axis=0, concat_axis=1, tiled=True)


def solution(mesh):
    in_specs = (
        P(("groups", "rows"), "cols"),
        P(None, "cols", "rows", None, None, None),
        P(None, "cols", "rows", None),
        P(None, "cols", "rows", None),
    )
    out_specs = P(("groups", "rows"), "cols")
    return jax.shard_map(
        on_device, mesh=mesh, in_specs=in_specs, out_specs=out_specs, check_vma=False
    )
```

time: 127 us -> 81.3 us (0.64)
  blocking collectives: 70.8 us -> 8.94 us
  between operations: 0.16 us -> 15.2 us
  starting transfers between devices: 34.9 us -> 26.3 us
  local copies, waits for them, and re-layouts: 1.53 us -> 9.97 us
  matrix products: 3.54 us -> 0.97 us
  waiting for transfers between devices: 14.5 us -> 16.4 us
  other arithmetic: 0.71 us -> 2.59 us
    all_to_all x7 -> x1, blocking collectives: 70.8 us -> 8.94 us  [on_device(): lax.all_to_all(block, 'rows', split_axis=0, concat_axis=1, tiled=True)]
    ppermute x20 -> x16, starting transfers between devices: 27.4 us -> 19 us  [the longest x12 18.8 us: shifted(): lax.ppermute(block, axis, [((i + distance) % size, i) for i in range(size)])]
    ppermute x20 -> x16, waiting for transfers between devices: 8.65 us -> 16.4 us  [the longest x12 15.2 us: shifted(): lax.ppermute(block, axis, [((i + distance) % size, i) for i in range(size)])]
    slice x1 -> x8, local copies, waits for them, and re-layouts: 0.73 us -> 7.99 us  [the longest x4 3 us: on_device(): jnp.roll(blocks, reach - m, axis=0)]
    all_to_all x1, waiting for transfers between devices: 5.85 us -> 0.01 us  [on_device(): lax.all_to_all(spread, 'rows', split_axis=0, concat_axis=0, tiled=True)]
    dot_general x4, matrix products: 3.54 us -> 0.97 us  [neuron_layer(): jnp.dot(stacked, weight_set.reshape(-1, weight_set.shape[-1]), preferred_...]
    unnamed x0 -> x22, other arithmetic: none -> 1.95 us
    unnamed x23 -> x4, local copies, waits for them, and re-layouts: 0.66 us -> 1.94 us
  transfers between devices with their start and end apart: 21 -> 17, of which waited for: 9 -> 4; matrix products, arithmetic and copies ran while one was open for 1% -> 6% of each run, Pallas kernels for 0% -> 0%
where the time goes in v1:
time: 81.3 us; the launch traced here: 80.3 us
  starting transfers between devices  26.3 us (32%)
  waiting for transfers between devices  16.4 us (20%)
  between operations  15.2 us (19%)
  local copies, waits for them, and re-layouts  9.97 us (12%)
  blocking collectives  8.94 us (11%)
  other arithmetic  2.59 us (3%)
  matrix products  0.97 us (1%)
    ppermute x12, starting transfers between devices, shifted(): lax.ppermute(block, axis, [((i + distance) % size, i) for i in range(size)])  18.8 us
    ppermute x12, waiting for transfers between devices, shifted(): lax.ppermute(block, axis, [((i + distance) % size, i) for i in range(size)])  15.2 us
    all_to_all x1, blocking collectives, on_device(): lax.all_to_all(block, 'rows', split_axis=0, concat_axis=1, tiled=True)  8.94 us
    all_to_all x1, starting transfers between devices, on_device(): lax.all_to_all(spread, 'rows', split_axis=0, concat_axis=0, tiled=True)  7.25 us
    slice x4, local copies, waits for them, and re-layouts, on_device(): jnp.roll(blocks, reach - m, axis=0)  3 us
    slice x2, local copies, waits for them, and re-layouts, neuron_layer(): active_set[m] > 0  2.93 us
    slice x1, local copies, waits for them, and re-layouts, on_device(): weights[layer, 0, 0]  2.05 us
    unnamed x22, other arithmetic  1.95 us
  transfers between devices with their start and end apart: 17, of which 4 were waited for; matrix products, arithmetic and copies ran while one was open for 6% of the time, Pallas kernels for 0%

profile of v1, /device:TPU:0, one launch (start us, length us, event | category | flops | bytes accessed | tf_op | source)
XLA Modules:
  0.0 80.3 jit_solution(6958247142552252664)
XLA Ops:
  0.0 0.7 fusion.13
  0.7 0.7 fusion.11
  1.4 0.8 fusion.10
  2.2 0.8 fusion.12
  3.0 0.6 constant_dynamic-update-slice_fusion.4
  3.6 0.6 constant_dynamic-update-slice_fusion.3
  4.2 1.3 %constant_dynamic-update-slice_fusion.2 = bf16[8,4,1280]{2,1,0:T(4,128)(2,1)} fusion(bf16[8,4,1280]{2,1,0:T(4,128)(2,1)} %constant_dynamic-update-slice_fusion.3, bf16[8,4,256]{2,1,0:T(4,128)(2,1)} %bitcast.54), kind=kLoop, calls=%fused_computation.14 | loop fusion | bytes 32768
  5.6 0.6 constant_dynamic-update-slice_fusion.1
  6.2 0.6 constant_dynamic-update-slice_fusion
  6.8 7.3 %all-to-all-start = ((bf16[8,4,1280]{2,1,0:T(4,128)(2,1)}), bf16[8,4,1280]{2,1,0:T(4,128)(2,1)S(1)}, u32[]{:S(2)}, u32[]{:S(2)}) async-start(bf16[8,4,1280]{2,1,0:T(4,128)(2,1)} %constant_dynamic-update-slice_fusion), calls=%async_computation | async-start | bytes 163840 | tf_op jit(solution)/shard_map/all_to_all | solution.py:31
  14.0 1.3 %fusion.16 = (s32[1,1,1,1]{3,2,1,0:T(1,128)}, s32[1,1,1,1]{3,2,1,0:T(1,128)}, s32[1,1,1,1]{3,2,1,0:T(1,128)}, s32[1,1,1,1]{3,2,1,0:T(1,128)}, s32[1,1,1,1]{3,2,1,0:T(1,128)}) fusion(s32[4,1,1,6]{3,2,1,0:T(1,128)} %param.6), kind=kLoop, calls=%fused_computation.53 | loop fusion | bytes 40 | tf_op jit(solution)/shard_map/slice | solution.py:17
  15.3 1.6 %fusion.15 = (s32[1,1,1,1]{3,2,1,0:T(1,128)}, s32[1,1,1,1]{3,2,1,0:T(1,128)}, s32[1,1,1,1]{3,2,1,0:T(1,128)}, s32[1,1,1,1]{3,2,1,0:T(1,128)}, s32[1,1,1,1]{3,2,1...) fusion(s32[4,1,1,6]{3,2,1,0:T(1,128)} %param.6), kind=kLoop, calls=%fused_computation.52 | loop fusion | bytes 152 | tf_op jit(solution)/shard_map/slice | solution.py:17
  20.7 0.0 copy-start
  20.7 2.1 %fusion.8 = (bf16[1,1,1,6,256,256]{5,4,3,2,1,0:T(8,128)(2,1)S(1)}, bf16[1,1,1,6,256,256]{5,4,3,2,1,0:T(8,128)(2,1)S(1)}, bf16[1,1,1,6,256,256]{5,4,3,2,1,0:T(8,128)(2,1)S(1)}, bf16[1,1,1,6,256,256]{5,4,3,2,1,0:T(8,128)(2,1)S(1)}) fusion(bf16[4,1,1,6,256,256]{5,4,3,2,1,0:T(8,128)(2,1)} %param.5), kind=kLoop, calls=%fused_computation.45 | loop fusion | bytes 6291456 | tf_op jit(solution)/shard_map/slice | solution.py:39
  22.8 0.0 copy-done
  22.8 0.0 all-to-all-done
  22.9 0.1 collective-permute-start
  23.0 1.1 %collective-permute-done = bf16[32,256]{1,0:T(8,128)(2,1)S(1)} collective-permute-done((bf16[32,256]{1,0:T(8,128)(2,1)S(1)}, bf16[32,256]{1,0:T(8,128)(2,1)S(1)}, u32[]{:S(2)}, u32[]{:S(2)}) %collective-permute-start) | collective-permute-done | bytes 16416 | tf_op jit(solution)/shard_map/ppermute | solution.py:13
  24.1 0.2 fusion.4
  24.4 2.1 %collective-permute-start.1 = (bf16[32,256]{1,0:T(8,128)(2,1)S(1)}, bf16[32,256]{1,0:T(8,128)(2,1)S(1)}, u32[]{:S(2)}, u32[]{:S(2)}) collective-permute-start(bf16[32,256]{1,0:T(8,128)(2,1)S(1)} %fusion.4), channel_id=1, source_target_pairs={{12,0},{14,2},{0,4},{2,6},{4,8},{6,10},{8,12},{10,14},{13,1},{15,3... | collective-permute-start | bytes 49160 | tf_op jit(solution)/shard_map/ppermute | solution.py:9
  30.1 0.1 collective-permute-start.5
  30.2 2.0 %collective-permute-start.4 = (bf16[32,256]{1,0:T(8,128)(2,1)S(1)}, bf16[32,256]{1,0:T(8,128)(2,1)S(1)}, u32[]{:S(2)}, u32[]{:S(2)}) collective-permute-start(bf16[32,256]{1,0:T(8,128)(2,1)S(1)} %fusion.4), channel_id=1, source_target_pairs={{4,0},{6,2},{8,4},{10,6},{12,8},{14,10},{0,12},{2,14},{5,1},{7,3},... | collective-permute-start | bytes 49160 | tf_op jit(solution)/shard_map/ppermute | solution.py:9
  32.2 2.8 %collective-permute-start.3 = (bf16[32,256]{1,0:T(8,128)(2,1)S(1)}, bf16[32,256]{1,0:T(8,128)(2,1)S(1)}, u32[]{:S(2)}, u32[]{:S(2)}) collective-permute-start(bf16[32,256]{1,0:T(8,128)(2,1)S(1)} %fusion.4), channel_id=1, source_target_pairs={{2,0},{4,2},{6,4},{8,6},{10,8},{12,10},{14,12},{0,14},{3,1},{5,3},... | collective-permute-start | bytes 49160 | tf_op jit(solution)/shard_map/ppermute | solution.py:9
  35.0 0.0 collective-permute-start.2
  35.0 0.0 collective-permute-done.1
  35.0 6.4 %collective-permute-done.2 = bf16[32,256]{1,0:T(8,128)(2,1)S(1)} collective-permute-done((bf16[32,256]{1,0:T(8,128)(2,1)S(1)}, bf16[32,256]{1,0:T(8,128)(2,1)S(1)}, u32[]{:S(2)}, u32[]{:S(2)}) %collective-permute-start.2) | collective-permute-done | bytes 16416 | tf_op jit(solution)/shard_map/ppermute | solution.py:9
  41.4 0.0 collective-permute-done.3
  41.5 0.0 collective-permute-done.4
  41.5 0.0 collective-permute-done.5
  41.5 0.2 fusion.5
  41.8 0.1 collective-permute-start.6
  45.5 0.1 collective-permute-start.10
  45.6 3.9 %collective-permute-start.9 = (bf16[32,256]{1,0:T(8,128)(2,1)S(1)}, bf16[32,256]{1,0:T(8,128)(2,1)S(1)}, u32[]{:S(2)}, u32[]{:S(2)}) collective-permute-start(bf16[32,256]{1,0:T(8,128)(2,1)S(1)} %fusion.5), channel_id=1, source_target_pairs={{4,0},{6,2},{8,4},{10,6},{12,8},{14,10},{0,12},{2,14},{5,1},{7,3},... | collective-permute-start | bytes 49160 | tf_op jit(solution)/shard_map/ppermute | solution.py:9
  49.5 0.0 collective-permute-start.8
  49.5 2.0 %collective-permute-start.7 = (bf16[32,256]{1,0:T(8,128)(2,1)S(1)}, bf16[32,256]{1,0:T(8,128)(2,1)S(1)}, u32[]{:S(2)}, u32[]{:S(2)}) collective-permute-start(bf16[32,256]{1,0:T(8,128)(2,1)S(1)} %fusion.5), channel_id=1, source_target_pairs={{14,0},{0,2},{2,4},{4,6},{6,8},{8,10},{10,12},{12,14},{15,1},{1,3}... | collective-permute-start | bytes 49160 | tf_op jit(solution)/shard_map/ppermute | solution.py:9
  51.5 0.0 collective-permute-done.6
  51.5 4.4 %collective-permute-done.7 = bf16[32,256]{1,0:T(8,128)(2,1)S(1)} collective-permute-done((bf16[32,256]{1,0:T(8,128)(2,1)S(1)}, bf16[32,256]{1,0:T(8,128)(2,1)S(1)}, u32[]{:S(2)}, u32[]{:S(2)}) %collective-permute-start.7) | collective-permute-done | bytes 16416 | tf_op jit(solution)/shard_map/ppermute | solution.py:9
  55.9 0.0 collective-permute-done.8
  56.0 0.0 collective-permute-done.9
  56.0 0.0 collective-permute-done.10
  56.0 0.2 fusion.6
  56.3 0.1 collective-permute-start.11
  60.0 0.1 collective-permute-start.15
  60.1 3.9 %collective-permute-start.14 = (bf16[32,256]{1,0:T(8,128)(2,1)S(1)}, bf16[32,256]{1,0:T(8,128)(2,1)S(1)}, u32[]{:S(2)}, u32[]{:S(2)}) collective-permute-start(bf16[32,256]{1,0:T(8,128)(2,1)S(1)} %fusion.6), channel_id=1, source_target_pairs={{4,0},{6,2},{8,4},{10,6},{12,8},{14,10},{0,12},{2,14},{5,1},{7,3},... | collective-permute-start | bytes 49160 | tf_op jit(solution)/shard_map/ppermute | solution.py:9
  64.0 0.0 collective-permute-start.13
  64.0 2.0 %collective-permute-start.12 = (bf16[32,256]{1,0:T(8,128)(2,1)S(1)}, bf16[32,256]{1,0:T(8,128)(2,1)S(1)}, u32[]{:S(2)}, u32[]{:S(2)}) collective-permute-start(bf16[32,256]{1,0:T(8,128)(2,1)S(1)} %fusion.6), channel_id=1, source_target_pairs={{14,0},{0,2},{2,4},{4,6},{6,8},{8,10},{10,12},{12,14},{15,1},{1,3}... | collective-permute-start | bytes 49160 | tf_op jit(solution)/shard_map/ppermute | solution.py:9
  66.0 0.0 collective-permute-done.11
  66.0 4.4 %collective-permute-done.12 = bf16[32,256]{1,0:T(8,128)(2,1)S(1)} collective-permute-done((bf16[32,256]{1,0:T(8,128)(2,1)S(1)}, bf16[32,256]{1,0:T(8,128)(2,1)S(1)}, u32[]{:S(2)}, u32[]{:S(2)}) %collective-permute-start.12) | collective-permute-done | bytes 16416 | tf_op jit(solution)/shard_map/ppermute | solution.py:9
  70.4 0.0 collective-permute-done.13
  70.5 0.0 collective-permute-done.14
  70.5 0.0 collective-permute-done.15
  70.5 0.2 fusion.7
  70.8 8.9 %all_to_all.24 = bf16[8,4,256]{2,1,0:T(4,128)(2,1)S(1)} all-to-all(bf16[8,4,256]{2,1,0:T(4,128)(2,1)S(1)} %all_to_all.18), channel_id=1, replica_groups=mesh['groups'=2,'rows'=8,'cols'=2] {'rows'}, dimensions={0} | all-to-all | bytes 32768 | tf_op jit(solution)/shard_map/all_to_all | solution.py:40
  79.7 0.6 copy.32
  (27 shorter events, 0.2 us)
Async XLA Ops:
  6.8 16.0 %all-to-all-start = ((bf16[8,4,1280]{2,1,0:T(4,128)(2,1)}), bf16[8,4,1280]{2,1,0:T(4,128)(2,1)S(1)}, u32[]{:S(2)}, u32[]{:S(2)}) async-start(bf16[8,4,1280]{2,1,0:T(4,128)(2,1)} %constant_dynamic-update-slice_fusion), calls=%async_computation | async-start | bytes 163840 | tf_op jit(solution)/shard_map/all_to_all | solution.py:31
  20.7 2.1 %copy-start = (f32[4,1,1,256]{3,2,1,0:T(1,128)S(1)}, f32[4,1,1,256]{3,2,1,0:T(1,128)}, u32[]{:S(2)}) copy-start(f32[4,1,1,256]{3,2,1,0:T(1,128)} %param.7) | copy-start | bytes 12292
  22.9 1.2 %collective-permute-start = (bf16[32,256]{1,0:T(8,128)(2,1)S(1)}, bf16[32,256]{1,0:T(8,128)(2,1)S(1)}, u32[]{:S(2)}, u32[]{:S(2)}) collective-permute-start(bf16[32,256]{1,0:T(8,128)(2,1)S(1)} %get-tuple-element.9), channel_id=1, source_target_pairs={{0,1},{1,0},{2,3},{3,2},{4,5},{5,4},{6,7},{7,6},{8,9},{9,8},{10,11... | collective-permute-start | bytes 49160 | tf_op jit(solution)/shard_map/ppermute | solution.py:13
  24.4 10.6 %collective-permute-start.1 = (bf16[32,256]{1,0:T(8,128)(2,1)S(1)}, bf16[32,256]{1,0:T(8,128)(2,1)S(1)}, u32[]{:S(2)}, u32[]{:S(2)}) collective-permute-start(bf16[32,256]{1,0:T(8,128)(2,1)S(1)} %fusion.4), channel_id=1, source_target_pairs={{12,0},{14,2},{0,4},{2,6},{4,8},{6,10},{8,12},{10,14},{13,1},{15,3... | collective-permute-start | bytes 49160 | tf_op jit(solution)/shard_map/ppermute | solution.py:9
  30.1 11.4 %collective-permute-start.5 = (bf16[32,256]{1,0:T(8,128)(2,1)S(1)}, bf16[32,256]{1,0:T(8,128)(2,1)S(1)}, u32[]{:S(2)}, u32[]{:S(2)}) collective-permute-start(bf16[32,256]{1,0:T(8,128)(2,1)S(1)} %fusion.4), channel_id=1, source_target_pairs={{0,1},{1,0},{2,3},{3,2},{4,5},{5,4},{6,7},{7,6},{8,9},{9,8},{10,11... | collective-permute-start | bytes 49160 | tf_op jit(solution)/shard_map/ppermute | solution.py:13
  30.2 11.3 %collective-permute-start.4 = (bf16[32,256]{1,0:T(8,128)(2,1)S(1)}, bf16[32,256]{1,0:T(8,128)(2,1)S(1)}, u32[]{:S(2)}, u32[]{:S(2)}) collective-permute-start(bf16[32,256]{1,0:T(8,128)(2,1)S(1)} %fusion.4), channel_id=1, source_target_pairs={{4,0},{6,2},{8,4},{10,6},{12,8},{14,10},{0,12},{2,14},{5,1},{7,3},... | collective-permute-start | bytes 49160 | tf_op jit(solution)/shard_map/ppermute | solution.py:9
  32.2 9.3 %collective-permute-start.3 = (bf16[32,256]{1,0:T(8,128)(2,1)S(1)}, bf16[32,256]{1,0:T(8,128)(2,1)S(1)}, u32[]{:S(2)}, u32[]{:S(2)}) collective-permute-start(bf16[32,256]{1,0:T(8,128)(2,1)S(1)} %fusion.4), channel_id=1, source_target_pairs={{2,0},{4,2},{6,4},{8,6},{10,8},{12,10},{14,12},{0,14},{3,1},{5,3},... | collective-permute-start | bytes 49160 | tf_op jit(solution)/shard_map/ppermute | solution.py:9
  35.0 6.4 %collective-permute-start.2 = (bf16[32,256]{1,0:T(8,128)(2,1)S(1)}, bf16[32,256]{1,0:T(8,128)(2,1)S(1)}, u32[]{:S(2)}, u32[]{:S(2)}) collective-permute-start(bf16[32,256]{1,0:T(8,128)(2,1)S(1)} %fusion.4), channel_id=1, source_target_pairs={{14,0},{0,2},{2,4},{4,6},{6,8},{8,10},{10,12},{12,14},{15,1},{1,3}... | collective-permute-start | bytes 49160 | tf_op jit(solution)/shard_map/ppermute | solution.py:9
  41.8 9.7 %collective-permute-start.6 = (bf16[32,256]{1,0:T(8,128)(2,1)S(1)}, bf16[32,256]{1,0:T(8,128)(2,1)S(1)}, u32[]{:S(2)}, u32[]{:S(2)}) collective-permute-start(bf16[32,256]{1,0:T(8,128)(2,1)S(1)} %fusion.5), channel_id=1, source_target_pairs={{12,0},{14,2},{0,4},{2,6},{4,8},{6,10},{8,12},{10,14},{13,1},{15,3... | collective-permute-start | bytes 49160 | tf_op jit(solution)/shard_map/ppermute | solution.py:9
  45.5 10.5 %collective-permute-start.10 = (bf16[32,256]{1,0:T(8,128)(2,1)S(1)}, bf16[32,256]{1,0:T(8,128)(2,1)S(1)}, u32[]{:S(2)}, u32[]{:S(2)}) collective-permute-start(bf16[32,256]{1,0:T(8,128)(2,1)S(1)} %fusion.5), channel_id=1, source_target_pairs={{0,1},{1,0},{2,3},{3,2},{4,5},{5,4},{6,7},{7,6},{8,9},{9,8},{10,11... | collective-permute-start | bytes 49160 | tf_op jit(solution)/shard_map/ppermute | solution.py:13
  45.6 10.4 %collective-permute-start.9 = (bf16[32,256]{1,0:T(8,128)(2,1)S(1)}, bf16[32,256]{1,0:T(8,128)(2,1)S(1)}, u32[]{:S(2)}, u32[]{:S(2)}) collective-permute-start(bf16[32,256]{1,0:T(8,128)(2,1)S(1)} %fusion.5), channel_id=1, source_target_pairs={{4,0},{6,2},{8,4},{10,6},{12,8},{14,10},{0,12},{2,14},{5,1},{7,3},... | collective-permute-start | bytes 49160 | tf_op jit(solution)/shard_map/ppermute | solution.py:9
  49.5 6.5 %collective-permute-start.8 = (bf16[32,256]{1,0:T(8,128)(2,1)S(1)}, bf16[32,256]{1,0:T(8,128)(2,1)S(1)}, u32[]{:S(2)}, u32[]{:S(2)}) collective-permute-start(bf16[32,256]{1,0:T(8,128)(2,1)S(1)} %fusion.5), channel_id=1, source_target_pairs={{2,0},{4,2},{6,4},{8,6},{10,8},{12,10},{14,12},{0,14},{3,1},{5,3},... | collective-permute-start | bytes 49160 | tf_op jit(solution)/shard_map/ppermute | solution.py:9
  49.5 6.4 %collective-permute-start.7 = (bf16[32,256]{1,0:T(8,128)(2,1)S(1)}, bf16[32,256]{1,0:T(8,128)(2,1)S(1)}, u32[]{:S(2)}, u32[]{:S(2)}) collective-permute-start(bf16[32,256]{1,0:T(8,128)(2,1)S(1)} %fusion.5), channel_id=1, source_target_pairs={{14,0},{0,2},{2,4},{4,6},{6,8},{8,10},{10,12},{12,14},{15,1},{1,3}... | collective-permute-start | bytes 49160 | tf_op jit(solution)/shard_map/ppermute | solution.py:9
  56.3 9.7 %collective-permute-start.11 = (bf16[32,256]{1,0:T(8,128)(2,1)S(1)}, bf16[32,256]{1,0:T(8,128)(2,1)S(1)}, u32[]{:S(2)}, u32[]{:S(2)}) collective-permute-start(bf16[32,256]{1,0:T(8,128)(2,1)S(1)} %fusion.6), channel_id=1, source_target_pairs={{12,0},{14,2},{0,4},{2,6},{4,8},{6,10},{8,12},{10,14},{13,1},{15,3... | collective-permute-start | bytes 49160 | tf_op jit(solution)/shard_map/ppermute | solution.py:9
  60.0 10.5 %collective-permute-start.15 = (bf16[32,256]{1,0:T(8,128)(2,1)S(1)}, bf16[32,256]{1,0:T(8,128)(2,1)S(1)}, u32[]{:S(2)}, u32[]{:S(2)}) collective-permute-start(bf16[32,256]{1,0:T(8,128)(2,1)S(1)} %fusion.6), channel_id=1, source_target_pairs={{0,1},{1,0},{2,3},{3,2},{4,5},{5,4},{6,7},{7,6},{8,9},{9,8},{10,11... | collective-permute-start | bytes 49160 | tf_op jit(solution)/shard_map/ppermute | solution.py:13
  60.1 10.4 %collective-permute-start.14 = (bf16[32,256]{1,0:T(8,128)(2,1)S(1)}, bf16[32,256]{1,0:T(8,128)(2,1)S(1)}, u32[]{:S(2)}, u32[]{:S(2)}) collective-permute-start(bf16[32,256]{1,0:T(8,128)(2,1)S(1)} %fusion.6), channel_id=1, source_target_pairs={{4,0},{6,2},{8,4},{10,6},{12,8},{14,10},{0,12},{2,14},{5,1},{7,3},... | collective-permute-start | bytes 49160 | tf_op jit(solution)/shard_map/ppermute | solution.py:9
  64.0 6.5 %collective-permute-start.13 = (bf16[32,256]{1,0:T(8,128)(2,1)S(1)}, bf16[32,256]{1,0:T(8,128)(2,1)S(1)}, u32[]{:S(2)}, u32[]{:S(2)}) collective-permute-start(bf16[32,256]{1,0:T(8,128)(2,1)S(1)} %fusion.6), channel_id=1, source_target_pairs={{2,0},{4,2},{6,4},{8,6},{10,8},{12,10},{14,12},{0,14},{3,1},{5,3},... | collective-permute-start | bytes 49160 | tf_op jit(solution)/shard_map/ppermute | solution.py:9
  64.0 6.4 %collective-permute-start.12 = (bf16[32,256]{1,0:T(8,128)(2,1)S(1)}, bf16[32,256]{1,0:T(8,128)(2,1)S(1)}, u32[]{:S(2)}, u32[]{:S(2)}) collective-permute-start(bf16[32,256]{1,0:T(8,128)(2,1)S(1)} %fusion.6), channel_id=1, source_target_pairs={{14,0},{0,2},{2,4},{4,6},{6,8},{8,10},{10,12},{12,14},{15,1},{1,3}... | collective-permute-start | bytes 49160 | tf_op jit(solution)/shard_map/ppermute | solution.py:9

commit v2 on v1

v2 whole, which is shorter than its diff:
```python
import functools

import jax
import jax.numpy as jnp
from jax import lax
from jax.experimental import pallas as pl
from jax.experimental.pallas import tpu as pltpu
from jax.sharding import PartitionSpec as P


def shifted(block, axis, distance):
    size = lax.axis_size(axis)
    return lax.ppermute(block, axis, [((i + distance) % size, i) for i in range(size)])


def partner(block):
    return lax.ppermute(block, "cols", [(i, i ^ 1) for i in range(lax.axis_size("cols"))])


def expand_kernel(reach, width, x_ref, o_ref):
    devices = o_ref.shape[0]
    for d in range(devices):
        for m in range(2 * reach + 1):
            source = (d + m - reach) % devices
            o_ref[d, :, m * width : (m + 1) * width] = x_ref[:, source * width : (source + 1) * width]


def expanded(features, devices, reach):
    samples, columns = features.shape
    width = columns // devices
    return pl.pallas_call(
        functools.partial(expand_kernel, reach, width),
        out_shape=jax.ShapeDtypeStruct((devices, samples, (2 * reach + 1) * width), features.dtype),
        in_specs=[pl.BlockSpec(memory_space=pltpu.VMEM)],
        out_specs=pl.BlockSpec(memory_space=pltpu.VMEM),
    )(features)


def neuron_layer(sources, weight_set, bias_row):
    stacked = jnp.concatenate(sources, axis=1)
    total = jnp.dot(stacked, weight_set, preferred_element_type=jnp.float32)
    return jnp.maximum(total + bias_row[None, :], 0.0).astype(jnp.bfloat16)


def on_device(features, weights, active, layer_bias):
    layer_count, _, _, candidates, width, _ = weights.shape
    reach = (candidates - 2) // 2
    devices = lax.axis_size("rows")
    samples = features.shape[0]

    spread = lax.all_to_all(expanded(features, devices, reach), "rows", split_axis=0, concat_axis=0, tiled=True)
    keep = active[:, 0, 0, :, None, None] > 0
    masked = jnp.where(keep, weights[:, 0, 0], jnp.zeros((), weights.dtype))
    masked = lax.optimization_barrier(masked.reshape(layer_count, candidates * width, width))

    spread = spread.reshape(devices * samples, (2 * reach + 1) * width)
    sources = [spread, partner(spread[:, reach * width : (reach + 1) * width])]
    order = [sign * step for sign in (1, -1) for step in range(reach, 0, -1)]
    for layer in range(layer_count):
        if layer:
            arrived = {0: block, None: partner(block)}
            for step in order:
                arrived[step] = shifted(block, "rows", step)
            sources = [arrived[m] for m in range(-reach, reach + 1)] + [arrived[None]]
        block = neuron_layer(sources, masked[layer], layer_bias[layer, 0, 0])
    return lax.all_to_all(block, "rows", split_axis=0, concat_axis=1, tiled=True)


def solution(mesh):
    in_specs = (
        P(("groups", "rows"), "cols"),
        P(None, "cols", "rows", None, None, None),
        P(None, "cols", "rows", None),
        P(None, "cols", "rows", None),
    )
    out_specs = P(("groups", "rows"), "cols")
    return jax.shard_map(
        on_device, mesh=mesh, in_specs=in_specs, out_specs=out_specs, check_vma=False
    )
```

time: 81.3 us -> 56.2 us (0.69)
  between operations: 15.2 us -> 0.23 us
  local copies, waits for them, and re-layouts: 9.97 us -> 0.8 us
  waiting for transfers between devices: 16.4 us -> 10.4 us
  blocking collectives: 8.94 us -> 10.4 us
  starting transfers between devices: 26.3 us -> 27.7 us
  Pallas kernels: 0 us -> 1.36 us
  other arithmetic: 2.59 us -> 3.89 us
    ppermute x12, waiting for transfers between devices: 15.2 us -> 6.29 us  [shifted(): lax.ppermute(block, axis, [((i + distance) % size, i) for i in range(size)])]
    slice x8 -> x2, local copies, waits for them, and re-layouts: 7.99 us -> 0.01 us  [the longest x1 0.01 us: on_device(): sources = [spread, partner(spread[:, reach * width:(reach + 1) * width])]]
    select_n x0 -> x1, other arithmetic: none -> 3.21 us  [on_device(): masked = jnp.where(keep, weights[:, 0, 0], jnp.zeros((), weights.dtype))]
    all_to_all x1, waiting for transfers between devices: 0.01 us -> 3 us  [on_device(): lax.all_to_all(expanded(features, devices, reach), 'rows', split_axis=0,...]
    unnamed x22 -> x0, other arithmetic: 1.95 us -> none
    ppermute x12, starting transfers between devices: 18.8 us -> 20.4 us  [shifted(): lax.ppermute(block, axis, [((i + distance) % size, i) for i in range(size)])]
    all_to_all x1, blocking collectives: 8.94 us -> 10.4 us  [on_device(): lax.all_to_all(block, 'rows', split_axis=0, concat_axis=1, tiled=True)]
    pallas_call x0 -> x1, Pallas kernels: none -> 1.36 us  [expanded(): pl.pallas_call(functools.partial(expand_kernel, reach, width), out_shape=...]
  transfers between devices with their start and end apart: 17 -> 17, of which waited for: 4 -> 6; matrix products, arithmetic and copies ran while one was open for 6% -> 7% of each run, Pallas kernels for 0% -> 0%
where the time goes in v2:
time: 56.2 us; the launch traced here: 55.8 us
  starting transfers between devices  27.7 us (49%)
  waiting for transfers between devices  10.4 us (19%)
  blocking collectives  10.4 us (19%)
  other arithmetic  3.89 us (7%)
  Pallas kernels  1.36 us (2%)
  matrix products  0.97 us (2%)
  local copies, waits for them, and re-layouts  0.8 us (1%)
    ppermute x12, starting transfers between devices, shifted(): lax.ppermute(block, axis, [((i + distance) % size, i) for i in range(size)])  20.4 us
    all_to_all x1, blocking collectives, on_device(): lax.all_to_all(block, 'rows', split_axis=0, concat_axis=1, tiled=True)  10.4 us
    all_to_all x1, starting transfers between devices, on_device(): lax.all_to_all(expanded(features, devices, reach), 'rows', split_axis=0,...  7.25 us
    ppermute x12, waiting for transfers between devices, shifted(): lax.ppermute(block, axis, [((i + distance) % size, i) for i in range(size)])  6.29 us
    select_n x1, other arithmetic, on_device(): masked = jnp.where(keep, weights[:, 0, 0], jnp.zeros((), weights.dtype))  3.21 us
    all_to_all x1, waiting for transfers between devices, on_device(): lax.all_to_all(expanded(features, devices, reach), 'rows', split_axis=0,...  3 us
    pallas_call x1, Pallas kernels, expanded(): pl.pallas_call(functools.partial(expand_kernel, reach, width), out_shape=...  1.36 us
    ppermute x4, waiting for transfers between devices, partner(): lax.ppermute(block, 'cols', [(i, i ^ 1) for i in range(lax.axis_size('col...  1.16 us
  transfers between devices with their start and end apart: 17, of which 6 were waited for; matrix products, arithmetic and copies ran while one was open for 7% of the time, Pallas kernels for 0%

profile of v2, /device:TPU:0, one launch (start us, length us, event | category | flops | bytes accessed | tf_op | source)
XLA Modules:
  0.0 55.8 jit_solution(3418924094839055026)
XLA Ops:
  0.0 1.4 %shard_map.46 = bf16[8,4,1280]{2,1,0:T(4,128)(2,1)} custom-call(bf16[4,2048]{1,0:T(4,128)(2,1)} %x_ref.1), custom_call_target="tpu_custom_call" | custom-call | tf_op jit(solution)/shard_map/pallas_call | solution.py:31
  1.4 7.3 %all-to-all-start = ((bf16[8,4,1280]{2,1,0:T(4,128)(2,1)}), bf16[8,4,1280]{2,1,0:T(4,128)(2,1)S(1)}, u32[]{:S(2)}, u32[]{:S(2)}) async-start(bf16[8,4,1280]{2,1,0:T(4,128)(2,1)} %shard_map.46), calls=%async_computation | async-start | bytes 163840 | tf_op jit(solution)/shard_map/all_to_all | solution.py:51
  8.6 0.7 %broadcast_compare_fusion = pred[4,1,1,6]{3,2,1,0:T(4,128)(4,1)S(1)} fusion(s32[4,1,1,6]{3,2,1,0:T(1,128)} %param.6), kind=kLoop, calls=%fused_computation.40 | loop fusion | flops 24 | bytes 120 | tf_op jit(solution)/shard_map/gt | solution.py:52
  9.3 0.1 broadcast_bitcast_fusion
  9.4 0.0 copy-start
  9.4 3.2 %bitcast_select_fusion = bf16[4,1536,256]{2,1,0:T(8,128)(2,1)S(1)} fusion(bf16[4,1,1,6,256,256]{5,4,3,2,1,0:T(8,128)(2,1)} %param.5, pred[4,1536]{1,0:T(4,128)(4,1)S(1)} %bitcast.31), kind=kLoop, calls=%fused_computation | loop fusion | flops 1572864 | bytes 6297600 | tf_op jit(solution)/shard_map/jit(_where)/select_n | solution.py:53
  12.6 3.0 %all-to-all-done = bf16[8,4,1280]{2,1,0:T(4,128)(2,1)S(1)} async-done(((bf16[8,4,1280]{2,1,0:T(4,128)(2,1)}), bf16[8,4,1280]{2,1,0:T(4,128)(2,1)S(1)}, u32[]{:S(2)}, u32[]{:S(2)}) %all-to-all-start) | async-done | bytes 81952 | tf_op jit(solution)/shard_map/all_to_all | solution.py:51
  15.7 0.1 collective-permute-start
  15.7 0.0 copy-done
  15.8 1.1 %collective-permute-done = bf16[32,256]{1,0:T(8,128)(2,1)S(1)} collective-permute-done((bf16[32,256]{1,0:T(8,128)(2,1)S(1)}, bf16[32,256]{1,0:T(8,128)(2,1)S(1)}, u32[]{:S(2)}, u32[]{:S(2)}) %collective-permute-start) | collective-permute-done | bytes 16416 | tf_op jit(solution)/shard_map/ppermute | solution.py:17
  16.9 0.2 fusion.4
  17.2 0.2 collective-permute-start.1
  17.3 1.1 %collective-permute-start.2 = (bf16[32,256]{1,0:T(8,128)(2,1)S(1)}, bf16[32,256]{1,0:T(8,128)(2,1)S(1)}, u32[]{:S(2)}, u32[]{:S(2)}) collective-permute-start(bf16[32,256]{1,0:T(8,128)(2,1)S(1)} %fusion.4), channel_id=1, source_target_pairs={{14,0},{0,2},{2,4},{4,6},{6,8},{8,10},{10,12},{12,14},{15,1},{1,3}... | collective-permute-start | bytes 49160 | tf_op jit(solution)/shard_map/ppermute | solution.py:13
  18.5 3.6 %collective-permute-start.3 = (bf16[32,256]{1,0:T(8,128)(2,1)S(1)}, bf16[32,256]{1,0:T(8,128)(2,1)S(1)}, u32[]{:S(2)}, u32[]{:S(2)}) collective-permute-start(bf16[32,256]{1,0:T(8,128)(2,1)S(1)} %fusion.4), channel_id=1, source_target_pairs={{2,0},{4,2},{6,4},{8,6},{10,8},{12,10},{14,12},{0,14},{3,1},{5,3},... | collective-permute-start | bytes 49160 | tf_op jit(solution)/shard_map/ppermute | solution.py:13
  22.1 1.9 %collective-permute-start.4 = (bf16[32,256]{1,0:T(8,128)(2,1)S(1)}, bf16[32,256]{1,0:T(8,128)(2,1)S(1)}, u32[]{:S(2)}, u32[]{:S(2)}) collective-permute-start(bf16[32,256]{1,0:T(8,128)(2,1)S(1)} %fusion.4), channel_id=1, source_target_pairs={{4,0},{6,2},{8,4},{10,6},{12,8},{14,10},{0,12},{2,14},{5,1},{7,3},... | collective-permute-start | bytes 49160 | tf_op jit(solution)/shard_map/ppermute | solution.py:13
  24.0 0.0 collective-permute-start.5
  24.0 0.0 collective-permute-done.1
  24.0 0.0 collective-permute-done.2
  24.0 0.0 collective-permute-done.3
  24.0 1.8 %collective-permute-done.4 = bf16[32,256]{1,0:T(8,128)(2,1)S(1)} collective-permute-done((bf16[32,256]{1,0:T(8,128)(2,1)S(1)}, bf16[32,256]{1,0:T(8,128)(2,1)S(1)}, u32[]{:S(2)}, u32[]{:S(2)}) %collective-permute-start.4) | collective-permute-done | bytes 16416 | tf_op jit(solution)/shard_map/ppermute | solution.py:13
  25.8 0.0 collective-permute-done.5
  25.8 0.2 fusion.5
  26.1 0.1 collective-permute-start.6
  26.1 0.1 collective-permute-start.7
  26.2 4.7 %collective-permute-start.8 = (bf16[32,256]{1,0:T(8,128)(2,1)S(1)}, bf16[32,256]{1,0:T(8,128)(2,1)S(1)}, u32[]{:S(2)}, u32[]{:S(2)}) collective-permute-start(bf16[32,256]{1,0:T(8,128)(2,1)S(1)} %fusion.5), channel_id=1, source_target_pairs={{2,0},{4,2},{6,4},{8,6},{10,8},{12,10},{14,12},{0,14},{3,1},{5,3},... | collective-permute-start | bytes 49160 | tf_op jit(solution)/shard_map/ppermute | solution.py:13
  30.9 2.0 %collective-permute-start.9 = (bf16[32,256]{1,0:T(8,128)(2,1)S(1)}, bf16[32,256]{1,0:T(8,128)(2,1)S(1)}, u32[]{:S(2)}, u32[]{:S(2)}) collective-permute-start(bf16[32,256]{1,0:T(8,128)(2,1)S(1)} %fusion.5), channel_id=1, source_target_pairs={{4,0},{6,2},{8,4},{10,6},{12,8},{14,10},{0,12},{2,14},{5,1},{7,3},... | collective-permute-start | bytes 49160 | tf_op jit(solution)/shard_map/ppermute | solution.py:13
  32.9 0.0 collective-permute-start.10
  32.9 0.0 collective-permute-done.6
  32.9 0.0 collective-permute-done.7
  32.9 0.0 collective-permute-done.8
  32.9 1.7 %collective-permute-done.9 = bf16[32,256]{1,0:T(8,128)(2,1)S(1)} collective-permute-done((bf16[32,256]{1,0:T(8,128)(2,1)S(1)}, bf16[32,256]{1,0:T(8,128)(2,1)S(1)}, u32[]{:S(2)}, u32[]{:S(2)}) %collective-permute-start.9) | collective-permute-done | bytes 16416 | tf_op jit(solution)/shard_map/ppermute | solution.py:13
  34.6 0.0 collective-permute-done.10
  34.7 0.2 fusion.6
  34.9 1.2 %collective-permute-start.11 = (bf16[32,256]{1,0:T(8,128)(2,1)S(1)}, bf16[32,256]{1,0:T(8,128)(2,1)S(1)}, u32[]{:S(2)}, u32[]{:S(2)}) collective-permute-start(bf16[32,256]{1,0:T(8,128)(2,1)S(1)} %fusion.6), channel_id=1, source_target_pairs={{12,0},{14,2},{0,4},{2,6},{4,8},{6,10},{8,12},{10,14},{13,1},{15,3... | collective-permute-start | bytes 49160 | tf_op jit(solution)/shard_map/ppermute | solution.py:13
  36.1 1.3 %collective-permute-start.12 = (bf16[32,256]{1,0:T(8,128)(2,1)S(1)}, bf16[32,256]{1,0:T(8,128)(2,1)S(1)}, u32[]{:S(2)}, u32[]{:S(2)}) collective-permute-start(bf16[32,256]{1,0:T(8,128)(2,1)S(1)} %fusion.6), channel_id=1, source_target_pairs={{14,0},{0,2},{2,4},{4,6},{6,8},{8,10},{10,12},{12,14},{15,1},{1,3}... | collective-permute-start | bytes 49160 | tf_op jit(solution)/shard_map/ppermute | solution.py:13
  37.4 3.4 %collective-permute-start.13 = (bf16[32,256]{1,0:T(8,128)(2,1)S(1)}, bf16[32,256]{1,0:T(8,128)(2,1)S(1)}, u32[]{:S(2)}, u32[]{:S(2)}) collective-permute-start(bf16[32,256]{1,0:T(8,128)(2,1)S(1)} %fusion.6), channel_id=1, source_target_pairs={{2,0},{4,2},{6,4},{8,6},{10,8},{12,10},{14,12},{0,14},{3,1},{5,3},... | collective-permute-start | bytes 49160 | tf_op jit(solution)/shard_map/ppermute | solution.py:13
  40.8 0.9 %collective-permute-start.14 = (bf16[32,256]{1,0:T(8,128)(2,1)S(1)}, bf16[32,256]{1,0:T(8,128)(2,1)S(1)}, u32[]{:S(2)}, u32[]{:S(2)}) collective-permute-start(bf16[32,256]{1,0:T(8,128)(2,1)S(1)} %fusion.6), channel_id=1, source_target_pairs={{4,0},{6,2},{8,4},{10,6},{12,8},{14,10},{0,12},{2,14},{5,1},{7,3},... | collective-permute-start | bytes 49160 | tf_op jit(solution)/shard_map/ppermute | solution.py:13
  41.7 0.0 collective-permute-start.15
  41.7 0.0 collective-permute-done.11
  41.7 0.8 %collective-permute-done.12 = bf16[32,256]{1,0:T(8,128)(2,1)S(1)} collective-permute-done((bf16[32,256]{1,0:T(8,128)(2,1)S(1)}, bf16[32,256]{1,0:T(8,128)(2,1)S(1)}, u32[]{:S(2)}, u32[]{:S(2)}) %collective-permute-start.12) | collective-permute-done | bytes 16416 | tf_op jit(solution)/shard_map/ppermute | solution.py:13
  42.5 0.0 collective-permute-done.13
  42.5 2.0 %collective-permute-done.14 = bf16[32,256]{1,0:T(8,128)(2,1)S(1)} collective-permute-done((bf16[32,256]{1,0:T(8,128)(2,1)S(1)}, bf16[32,256]{1,0:T(8,128)(2,1)S(1)}, u32[]{:S(2)}, u32[]{:S(2)}) %collective-permute-start.14) | collective-permute-done | bytes 16416 | tf_op jit(solution)/shard_map/ppermute | solution.py:13
  44.5 0.0 collective-permute-done.15
  44.5 0.2 fusion.7
  44.8 10.4 %all_to_all.24 = bf16[8,4,256]{2,1,0:T(4,128)(2,1)S(1)} all-to-all(bf16[8,4,256]{2,1,0:T(4,128)(2,1)S(1)} %all_to_all.18), channel_id=1, replica_groups=mesh['groups'=2,'rows'=8,'cols'=2] {'rows'}, dimensions={0} | all-to-all | bytes 32768 | tf_op jit(solution)/shard_map/all_to_all | solution.py:66
  55.2 0.6 %copy.27 = bf16[4,2048]{1,0:T(4,128)(2,1)} copy(bf16[4,2048]{1,0:T(4,128)(2,1)S(1)} %bitcast.30) | data formatting | bytes 32768
  (24 shorter events, 0.1 us)
Async XLA Ops:
  1.4 14.3 %all-to-all-start = ((bf16[8,4,1280]{2,1,0:T(4,128)(2,1)}), bf16[8,4,1280]{2,1,0:T(4,128)(2,1)S(1)}, u32[]{:S(2)}, u32[]{:S(2)}) async-start(bf16[8,4,1280]{2,1,0:T(4,128)(2,1)} %shard_map.46), calls=%async_computation | async-start | bytes 163840 | tf_op jit(solution)/shard_map/all_to_all | solution.py:51
  9.4 6.3 %copy-start = (f32[4,1,1,256]{3,2,1,0:T(1,128)S(1)}, f32[4,1,1,256]{3,2,1,0:T(1,128)}, u32[]{:S(2)}) copy-start(f32[4,1,1,256]{3,2,1,0:T(1,128)} %param.7) | copy-start | bytes 12292
  15.7 1.2 %collective-permute-start = (bf16[32,256]{1,0:T(8,128)(2,1)S(1)}, bf16[32,256]{1,0:T(8,128)(2,1)S(1)}, u32[]{:S(2)}, u32[]{:S(2)}) collective-permute-start(bf16[32,256]{1,0:T(8,128)(2,1)S(1)} %slice.36), channel_id=1, source_target_pairs={{0,1},{1,0},{2,3},{3,2},{4,5},{5,4},{6,7},{7,6},{8,9},{9,8},{10,11... | collective-permute-start | bytes 49160 | tf_op jit(solution)/shard_map/ppermute | solution.py:17
  17.2 6.8 %collective-permute-start.1 = (bf16[32,256]{1,0:T(8,128)(2,1)S(1)}, bf16[32,256]{1,0:T(8,128)(2,1)S(1)}, u32[]{:S(2)}, u32[]{:S(2)}) collective-permute-start(bf16[32,256]{1,0:T(8,128)(2,1)S(1)} %fusion.4), channel_id=1, source_target_pairs={{12,0},{14,2},{0,4},{2,6},{4,8},{6,10},{8,12},{10,14},{13,1},{15,3... | collective-permute-start | bytes 49160 | tf_op jit(solution)/shard_map/ppermute | solution.py:13
  17.3 6.6 %collective-permute-start.2 = (bf16[32,256]{1,0:T(8,128)(2,1)S(1)}, bf16[32,256]{1,0:T(8,128)(2,1)S(1)}, u32[]{:S(2)}, u32[]{:S(2)}) collective-permute-start(bf16[32,256]{1,0:T(8,128)(2,1)S(1)} %fusion.4), channel_id=1, source_target_pairs={{14,0},{0,2},{2,4},{4,6},{6,8},{8,10},{10,12},{12,14},{15,1},{1,3}... | collective-permute-start | bytes 49160 | tf_op jit(solution)/shard_map/ppermute | solution.py:13
  18.5 5.6 %collective-permute-start.3 = (bf16[32,256]{1,0:T(8,128)(2,1)S(1)}, bf16[32,256]{1,0:T(8,128)(2,1)S(1)}, u32[]{:S(2)}, u32[]{:S(2)}) collective-permute-start(bf16[32,256]{1,0:T(8,128)(2,1)S(1)} %fusion.4), channel_id=1, source_target_pairs={{2,0},{4,2},{6,4},{8,6},{10,8},{12,10},{14,12},{0,14},{3,1},{5,3},... | collective-permute-start | bytes 49160 | tf_op jit(solution)/shard_map/ppermute | solution.py:13
  22.1 3.7 %collective-permute-start.4 = (bf16[32,256]{1,0:T(8,128)(2,1)S(1)}, bf16[32,256]{1,0:T(8,128)(2,1)S(1)}, u32[]{:S(2)}, u32[]{:S(2)}) collective-permute-start(bf16[32,256]{1,0:T(8,128)(2,1)S(1)} %fusion.4), channel_id=1, source_target_pairs={{4,0},{6,2},{8,4},{10,6},{12,8},{14,10},{0,12},{2,14},{5,1},{7,3},... | collective-permute-start | bytes 49160 | tf_op jit(solution)/shard_map/ppermute | solution.py:13
  24.0 1.8 %collective-permute-start.5 = (bf16[32,256]{1,0:T(8,128)(2,1)S(1)}, bf16[32,256]{1,0:T(8,128)(2,1)S(1)}, u32[]{:S(2)}, u32[]{:S(2)}) collective-permute-start(bf16[32,256]{1,0:T(8,128)(2,1)S(1)} %fusion.4), channel_id=1, source_target_pairs={{0,1},{1,0},{2,3},{3,2},{4,5},{5,4},{6,7},{7,6},{8,9},{9,8},{10,11... | collective-permute-start | bytes 49160 | tf_op jit(solution)/shard_map/ppermute | solution.py:17
  26.1 6.8 %collective-permute-start.6 = (bf16[32,256]{1,0:T(8,128)(2,1)S(1)}, bf16[32,256]{1,0:T(8,128)(2,1)S(1)}, u32[]{:S(2)}, u32[]{:S(2)}) collective-permute-start(bf16[32,256]{1,0:T(8,128)(2,1)S(1)} %fusion.5), channel_id=1, source_target_pairs={{12,0},{14,2},{0,4},{2,6},{4,8},{6,10},{8,12},{10,14},{13,1},{15,3... | collective-permute-start | bytes 49160 | tf_op jit(solution)/shard_map/ppermute | solution.py:13
  26.1 6.8 %collective-permute-start.7 = (bf16[32,256]{1,0:T(8,128)(2,1)S(1)}, bf16[32,256]{1,0:T(8,128)(2,1)S(1)}, u32[]{:S(2)}, u32[]{:S(2)}) collective-permute-start(bf16[32,256]{1,0:T(8,128)(2,1)S(1)} %fusion.5), channel_id=1, source_target_pairs={{14,0},{0,2},{2,4},{4,6},{6,8},{8,10},{10,12},{12,14},{15,1},{1,3}... | collective-permute-start | bytes 49160 | tf_op jit(solution)/shard_map/ppermute | solution.py:13
  26.2 6.7 %collective-permute-start.8 = (bf16[32,256]{1,0:T(8,128)(2,1)S(1)}, bf16[32,256]{1,0:T(8,128)(2,1)S(1)}, u32[]{:S(2)}, u32[]{:S(2)}) collective-permute-start(bf16[32,256]{1,0:T(8,128)(2,1)S(1)} %fusion.5), channel_id=1, source_target_pairs={{2,0},{4,2},{6,4},{8,6},{10,8},{12,10},{14,12},{0,14},{3,1},{5,3},... | collective-permute-start | bytes 49160 | tf_op jit(solution)/shard_map/ppermute | solution.py:13
  30.9 3.7 %collective-permute-start.9 = (bf16[32,256]{1,0:T(8,128)(2,1)S(1)}, bf16[32,256]{1,0:T(8,128)(2,1)S(1)}, u32[]{:S(2)}, u32[]{:S(2)}) collective-permute-start(bf16[32,256]{1,0:T(8,128)(2,1)S(1)} %fusion.5), channel_id=1, source_target_pairs={{4,0},{6,2},{8,4},{10,6},{12,8},{14,10},{0,12},{2,14},{5,1},{7,3},... | collective-permute-start | bytes 49160 | tf_op jit(solution)/shard_map/ppermute | solution.py:13
  32.9 1.8 %collective-permute-start.10 = (bf16[32,256]{1,0:T(8,128)(2,1)S(1)}, bf16[32,256]{1,0:T(8,128)(2,1)S(1)}, u32[]{:S(2)}, u32[]{:S(2)}) collective-permute-start(bf16[32,256]{1,0:T(8,128)(2,1)S(1)} %fusion.5), channel_id=1, source_target_pairs={{0,1},{1,0},{2,3},{3,2},{4,5},{5,4},{6,7},{7,6},{8,9},{9,8},{10,11... | collective-permute-start | bytes 49160 | tf_op jit(solution)/shard_map/ppermute | solution.py:17
  34.9 6.8 %collective-permute-start.11 = (bf16[32,256]{1,0:T(8,128)(2,1)S(1)}, bf16[32,256]{1,0:T(8,128)(2,1)S(1)}, u32[]{:S(2)}, u32[]{:S(2)}) collective-permute-start(bf16[32,256]{1,0:T(8,128)(2,1)S(1)} %fusion.6), channel_id=1, source_target_pairs={{12,0},{14,2},{0,4},{2,6},{4,8},{6,10},{8,12},{10,14},{13,1},{15,3... | collective-permute-start | bytes 49160 | tf_op jit(solution)/shard_map/ppermute | solution.py:13
  36.1 6.4 %collective-permute-start.12 = (bf16[32,256]{1,0:T(8,128)(2,1)S(1)}, bf16[32,256]{1,0:T(8,128)(2,1)S(1)}, u32[]{:S(2)}, u32[]{:S(2)}) collective-permute-start(bf16[32,256]{1,0:T(8,128)(2,1)S(1)} %fusion.6), channel_id=1, source_target_pairs={{14,0},{0,2},{2,4},{4,6},{6,8},{8,10},{10,12},{12,14},{15,1},{1,3}... | collective-permute-start | bytes 49160 | tf_op jit(solution)/shard_map/ppermute | solution.py:13
  37.4 5.1 %collective-permute-start.13 = (bf16[32,256]{1,0:T(8,128)(2,1)S(1)}, bf16[32,256]{1,0:T(8,128)(2,1)S(1)}, u32[]{:S(2)}, u32[]{:S(2)}) collective-permute-start(bf16[32,256]{1,0:T(8,128)(2,1)S(1)} %fusion.6), channel_id=1, source_target_pairs={{2,0},{4,2},{6,4},{8,6},{10,8},{12,10},{14,12},{0,14},{3,1},{5,3},... | collective-permute-start | bytes 49160 | tf_op jit(solution)/shard_map/ppermute | solution.py:13
  40.8 3.7 %collective-permute-start.14 = (bf16[32,256]{1,0:T(8,128)(2,1)S(1)}, bf16[32,256]{1,0:T(8,128)(2,1)S(1)}, u32[]{:S(2)}, u32[]{:S(2)}) collective-permute-start(bf16[32,256]{1,0:T(8,128)(2,1)S(1)} %fusion.6), channel_id=1, source_target_pairs={{4,0},{6,2},{8,4},{10,6},{12,8},{14,10},{0,12},{2,14},{5,1},{7,3},... | collective-permute-start | bytes 49160 | tf_op jit(solution)/shard_map/ppermute | solution.py:13
  41.7 2.8 %collective-permute-start.15 = (bf16[32,256]{1,0:T(8,128)(2,1)S(1)}, bf16[32,256]{1,0:T(8,128)(2,1)S(1)}, u32[]{:S(2)}, u32[]{:S(2)}) collective-permute-start(bf16[32,256]{1,0:T(8,128)(2,1)S(1)} %fusion.6), channel_id=1, source_target_pairs={{0,1},{1,0},{2,3},{3,2},{4,5},{5,4},{6,7},{7,6},{8,9},{9,8},{10,11... | collective-permute-start | bytes 49160 | tf_op jit(solution)/shard_map/ppermute | solution.py:17

commit v3 on v2

v3 whole, which is shorter than its diff:
```python
import functools

import jax
import jax.numpy as jnp
import numpy as np
from jax import lax
from jax.experimental import pallas as pl
from jax.experimental.pallas import tpu as pltpu
from jax.sharding import PartitionSpec as P


FAR, NEAR = 0, 1


def step_to(cycle, core, r, rows, where):
    if cycle == FAR:
        before = where(r <= 1, -2, where(r == rows - 1, 1, -1))
        after = where(r == 0, -1, where(r >= rows - 2, 2, 1))
    else:
        even = r % 2 == 0
        before = where(even, where(r == 0, 1, -2), where(r == rows - 1, -1, 2))
        after = where(even, where(r == rows - 2, 1, 2), where(r == 1, -1, -2))
    return where(core == 0, before, after)


def from_source(value, cycle):
    rows, cols = lax.axis_size("rows"), lax.axis_size("cols")
    pairs = []
    for r in range(rows):
        for c in range(cols):
            source = (r + int(step_to(cycle, c, r, rows, np.where))) % rows
            pairs.append((source * cols + c, r * cols + c))
    return lax.ppermute(value, ("rows", "cols"), pairs)


def partner(value):
    return lax.ppermute(value, "cols", [(i, i ^ 1) for i in range(lax.axis_size("cols"))])


def expand_kernel(reach, width, x_ref, o_ref):
    rows = o_ref.shape[0]
    for r in range(rows):
        for m in range(2 * reach + 1):
            source = (r + m - reach) % rows
            o_ref[r, :, m * width : (m + 1) * width] = x_ref[:, source * width : (source + 1) * width]


def expanded(features, rows, reach):
    samples, columns = features.shape
    width = columns // rows
    return pl.pallas_call(
        functools.partial(expand_kernel, reach, width),
        out_shape=pltpu.VMEM((rows, samples, (2 * reach + 1) * width), features.dtype),
        in_specs=[pl.BlockSpec(memory_space=pltpu.VMEM)],
        out_specs=pl.BlockSpec(memory_space=pltpu.VMEM),
    )(features)


def weight_kernel(plan, rows, active_ref, w_ref, *refs):
    outs, arrived = refs[:-1], refs[-1]
    width = w_ref.shape[-1]
    core, row = lax.axis_index("cols"), lax.axis_index("rows")
    copies = []
    for out, layer, sources in plan:
        for place, source in enumerate(sources):
            m = source(core, row)
            target = outs[out].at[pl.ds(place * width, width), :]
            copy = pltpu.make_async_copy(w_ref.at[layer, m], target, arrived.at[len(copies)])
            copy.start()
            copies.append((copy, layer, m, target))
    for copy, layer, m, target in copies:
        copy.wait()

        @pl.when(active_ref[layer, m] == 0)
        def _():
            target[...] = jnp.zeros_like(target)


def kept_weights(weights, active, reach, rows):
    layer_count, candidates, width, _ = weights.shape
    fixed = lambda m: lambda core, row: m
    taken = lambda cycle: lambda core, row: reach + step_to(cycle, core, row, rows, jnp.where)
    given = lambda cycle: lambda core, row: reach + step_to(cycle, 1 - core, row, rows, jnp.where)
    cycles = (FAR, NEAR)
    plan = [(0, 0, [fixed(m) for m in range(candidates - 1)]), (1, 0, [fixed(candidates - 1)])]
    for layer in range(1, layer_count):
        plan.append((len(plan), layer, [given(cycle) for cycle in cycles]))
        plan.append((len(plan), layer, [fixed(reach), fixed(candidates - 1)] + [taken(cycle) for cycle in cycles]))
    blocks = sum(len(sources) for _, _, sources in plan)
    return pl.pallas_call(
        functools.partial(weight_kernel, plan, rows),
        out_shape=[pltpu.VMEM((len(sources) * width, width), weights.dtype) for _, _, sources in plan],
        in_specs=[pl.BlockSpec(memory_space=pltpu.SMEM), pl.BlockSpec(memory_space=pl.ANY)],
        out_specs=[pl.BlockSpec(memory_space=pltpu.VMEM) for _ in plan],
        scratch_shapes=[pltpu.SemaphoreType.DMA((blocks,))],
        cost_estimate=pl.CostEstimate(flops=0, bytes_accessed=2 * weights.size * 2, transcendentals=0),
    )(active, weights)


def on_device(features, weights, active, layer_bias):
    layer_count, _, _, candidates, width, _ = weights.shape
    reach = (candidates - 2) // 2
    rows, cols = lax.axis_size("rows"), lax.axis_size("cols")
    core = lax.axis_index("cols")
    samples = features.shape[0]

    spread = lax.all_to_all(expanded(features, rows, reach), "rows", split_axis=0, concat_axis=0, tiled=True)
    kept = kept_weights(weights[:, 0, 0], active[:, 0, 0], reach, rows)
    for_own = kept[0:1] + kept[3::2]
    for_other = [partner(w) for w in kept[1:2] + kept[2::2]]

    spread = spread.reshape(rows * samples, (2 * reach + 1) * width)
    for layer in range(layer_count):
        if layer:
            both = jnp.concatenate([own, other], axis=1)
            again = lax.optimization_barrier(jnp.concatenate(lax.optimization_barrier([own, other]), axis=1))
            arrived = [both, from_source(both, FAR), from_source(again, NEAR)]
            own, other = [x[:, :width] for x in arrived], [x[:, width:] for x in arrived]
            to_own = jnp.concatenate([own[0], other[0]] + own[1:], axis=1)
            to_other = jnp.concatenate(other[1:], axis=1)
        else:
            to_own, to_other = spread, spread[:, reach * width : (reach + 1) * width]
        part_own = jnp.dot(to_own, for_own[layer], preferred_element_type=jnp.float32)
        part_own = part_own + layer_bias[layer, 0, 0][None, :]
        part_other = jnp.dot(to_other, for_other[layer], preferred_element_type=jnp.float32)
        if layer < layer_count - 1:
            far = partner(jnp.concatenate([part_own, part_other], axis=1))
            own = jnp.maximum(part_own + far[:, width:], 0.0).astype(jnp.bfloat16)
            other = jnp.maximum(part_other + far[:, :width], 0.0).astype(jnp.bfloat16)
    shape = (rows, samples, width)
    by_half = [jnp.where(core == h, part_own, part_other).reshape(shape) for h in range(cols)]
    parts = jnp.stack(by_half, axis=1).reshape(rows * cols, samples, width)
    parts = lax.all_to_all(parts, ("rows", "cols"), split_axis=0, concat_axis=0, tiled=True)
    total = parts.reshape(rows, cols, samples, width).sum(axis=1)
    return jnp.maximum(total, 0.0).astype(jnp.bfloat16).transpose(1, 0, 2).reshape(samples, rows * width)


def solution(mesh):
    in_specs = (
        P(("groups", "rows"), "cols"),
        P(None, "cols", "rows", None, None, None),
        P(None, "cols", "rows", None),
        P(None, "cols", "rows", None),
    )
    out_specs = P(("groups", "rows"), "cols")
    return jax.shard_map(
        on_device, mesh=mesh, in_specs=in_specs, out_specs=out_specs, check_vma=False
    )
```

time: 56.2 us -> 52.1 us (0.927)
  starting transfers between devices: 27.7 us -> 16.1 us
  waiting for transfers between devices: 10.4 us -> 18.2 us
  other arithmetic: 3.89 us -> 0.73 us
  Pallas kernels: 1.36 us -> 4.2 us
  local copies, waits for them, and re-layouts: 0.8 us -> 0.08 us
    ppermute x16 -> x13, starting transfers between devices: 20.5 us -> 8.85 us  [the longest x6 7.11 us: from_source(): return lax.ppermute(value, ('rows', 'cols'), pairs)]
    ppermute x16 -> x13, waiting for transfers between devices: 7.45 us -> 14.1 us  [the longest x6 11.9 us: from_source(): return lax.ppermute(value, ('rows', 'cols'), pairs)]
    select_n x1 -> x0, other arithmetic: 3.21 us -> none  [on_device(): masked = jnp.where(keep, weights[:, 0, 0], jnp.zeros((), weights.dtype))]
    pallas_call x0 -> x1, Pallas kernels: none -> 2.82 us  [kept_weights(): pl.pallas_call(functools.partial(weight_kernel, plan, rows), out_shape=[p...]
    all_to_all x1, waiting for transfers between devices: 3 us -> 4.08 us  [on_device(): lax.all_to_all(expanded(features, rows, reach), 'rows', split_axis=0, con...]
    unnamed x21 -> x2, local copies, waits for them, and re-layouts: 0.75 us -> 0.01 us
    gt x1 -> x0, other arithmetic: 0.69 us -> none  [on_device(): keep = active[:, 0, 0, :, None, None] > 0]
    convert_element_type x0 -> x4, other arithmetic: none -> 0.65 us  [the longest x1 0.62 us: on_device(): jnp.maximum(total, 0.0).astype(jnp.bfloat16).transpose(1, 0, 2)]
  transfers between devices with their start and end apart: 17 -> 14, of which waited for: 6 -> 9; matrix products, arithmetic and copies ran while one was open for 7% -> 1% of each run, Pallas kernels for 0% -> 5%
where the time goes in v3:
time: 52.1 us; the launch traced here: 51.7 us
  waiting for transfers between devices  18.2 us (35%)
  starting transfers between devices  16.1 us (31%)
  blocking collectives  10.8 us (21%)
  Pallas kernels  4.2 us (8%)
  matrix products  1.4 us (3%)
  other arithmetic  0.73 us (1%)
    ppermute x6, waiting for transfers between devices, from_source(): return lax.ppermute(value, ('rows', 'cols'), pairs)  11.9 us
    all_to_all x1, blocking collectives, on_device(): lax.all_to_all(parts, ('rows', 'cols'), split_axis=0, concat_axis=0, tile...  10.8 us
    all_to_all x1, starting transfers between devices, on_device(): lax.all_to_all(expanded(features, rows, reach), 'rows', split_axis=0, con...  7.25 us
    ppermute x6, starting transfers between devices, from_source(): return lax.ppermute(value, ('rows', 'cols'), pairs)  7.11 us
    all_to_all x1, waiting for transfers between devices, on_device(): lax.all_to_all(expanded(features, rows, reach), 'rows', split_axis=0, con...  4.08 us
    pallas_call x1, Pallas kernels, kept_weights(): pl.pallas_call(functools.partial(weight_kernel, plan, rows), out_shape=[p...  2.82 us
    ppermute x7, waiting for transfers between devices, partner(): lax.ppermute(value, 'cols', [(i, i ^ 1) for i in range(lax.axis_size('col...  2.24 us
    ppermute x7, starting transfers between devices, partner(): lax.ppermute(value, 'cols', [(i, i ^ 1) for i in range(lax.axis_size('col...  1.74 us
  transfers between devices with their start and end apart: 14, of which 9 were waited for; matrix products, arithmetic and copies ran while one was open for 1% of the time, Pallas kernels for 5%

profile of v3, /device:TPU:0, one launch (start us, length us, event | category | flops | bytes accessed | tf_op | source)
XLA Modules:
  0.0 51.7 jit_solution(7622872565976655229)
XLA Ops:
  0.0 0.0 copy-start
  0.0 1.4 %shard_map.47 = bf16[8,4,1280]{2,1,0:T(4,128)(2,1)} custom-call(bf16[4,2048]{1,0:T(4,128)(2,1)} %x_ref.1), custom_call_target="tpu_custom_call" | custom-call | tf_op jit(solution)/shard_map/pallas_call | solution.py:51
  1.4 7.3 %all-to-all-start = ((bf16[8,4,1280]{2,1,0:T(4,128)(2,1)}), bf16[8,4,1280]{2,1,0:T(4,128)(2,1)S(1)}, u32[]{:S(2)}, u32[]{:S(2)}) async-start(bf16[8,4,1280]{2,1,0:T(4,128)(2,1)} %shard_map.47), calls=%async_computation | async-start | bytes 163840 | tf_op jit(solution)/shard_map/all_to_all | solution.py:107
  8.6 2.8 %shard_map.46 = (bf16[1280,256]{1,0:T(8,128)(2,1)S(1)}, bf16[256,256]{1,0:T(8,128)(2,1)S(1)}, bf16[512,256]{1,0:T(8,128)(2,1)S(1)}, bf16[1024,256]{1,0:T(8,128)(...) custom-call(s32[4,6]{1,0:T(4,128)} %bitcast.35, ...), custom_call_target="tpu_custom_call" | custom-call | bytes 6291456 | tf_op jit(solution)/shard_map/pallas_call | solution.py:90
  11.5 0.1 collective-permute-start
  11.5 0.0 copy-done
  11.6 4.1 %all-to-all-done = bf16[8,4,1280]{2,1,0:T(4,128)(2,1)S(1)} async-done(((bf16[8,4,1280]{2,1,0:T(4,128)(2,1)}), bf16[8,4,1280]{2,1,0:T(4,128)(2,1)S(1)}, u32[]{:S(2)}, u32[]{:S(2)}) %all-to-all-start) | async-done | bytes 81952 | tf_op jit(solution)/shard_map/all_to_all | solution.py:107
  15.7 0.2 fusion
  15.9 0.0 collective-permute-done
  15.9 0.2 convolution_bitcast_fusion
  16.1 0.0 collective-permute-start.1
  16.1 0.5 collective-permute-start.4
  16.6 0.7 %collective-permute-done.1 = f32[32,512]{1,0:T(8,128)S(1)} collective-permute-done((f32[32,512]{1,0:T(8,128)S(1)}, f32[32,512]{1,0:T(8,128)S(1)}, u32[]{:S(2)}, u32[]{:S(2)}) %collective-permute-start.1) | collective-permute-done | bytes 65568 | tf_op jit(solution)/shard_map/ppermute | solution.py:37
  17.4 1.7 %collective-permute-start.2 = (bf16[32,512]{1,0:T(8,128)(2,1)S(1)}, bf16[32,512]{1,0:T(8,128)(2,1)S(1)}, u32[]{:S(2)}, u32[]{:S(2)}) collective-permute-start(bf16[32,512]{1,0:T(8,128)(2,1)S(1)} %pad_maximum_fusion.4), channel_id=1, source_target_pairs={{12,0},{15,1},{14,2},{5,3},{2,4},{7,5},{4,6},{9,7},{6,8},{11,9},{8... | collective-permute-start | bytes 98312 | tf_op jit(solution)/shard_map/ppermute | solution.py:33
  19.1 0.0 collective-permute-start.3
  19.1 4.0 %collective-permute-done.2 = bf16[32,512]{1,0:T(8,128)(2,1)S(1)} collective-permute-done((bf16[32,512]{1,0:T(8,128)(2,1)S(1)}, bf16[32,512]{1,0:T(8,128)(2,1)S(1)}, u32[]{:S(2)}, u32[]{:S(2)}) %collective-permute-start.2) | collective-permute-done | bytes 32800 | tf_op jit(solution)/shard_map/ppermute | solution.py:33
  23.1 0.0 collective-permute-done.3
  23.1 0.2 convolution_add_fusion.3
  23.3 0.0 collective-permute-done.4
  23.4 0.1 fusion.34
  23.5 0.3 collective-permute-start.5
  23.8 0.3 collective-permute-start.8
  24.1 0.7 %collective-permute-done.5 = f32[32,512]{1,0:T(8,128)S(1)} collective-permute-done((f32[32,512]{1,0:T(8,128)S(1)}, f32[32,512]{1,0:T(8,128)S(1)}, u32[]{:S(2)}, u32[]{:S(2)}) %collective-permute-start.5) | collective-permute-done | bytes 65568 | tf_op jit(solution)/shard_map/ppermute | solution.py:37
  24.9 2.6 %collective-permute-start.6 = (bf16[32,512]{1,0:T(8,128)(2,1)S(1)}, bf16[32,512]{1,0:T(8,128)(2,1)S(1)}, u32[]{:S(2)}, u32[]{:S(2)}) collective-permute-start(bf16[32,512]{1,0:T(8,128)(2,1)S(1)} %pad_maximum_fusion.6), channel_id=1, source_target_pairs={{12,0},{15,1},{14,2},{5,3},{2,4},{7,5},{4,6},{9,7},{6,8},{11,9},{8... | collective-permute-start | bytes 98312 | tf_op jit(solution)/shard_map/ppermute | solution.py:33
  27.5 0.0 collective-permute-start.7
  27.5 3.1 %collective-permute-done.6 = bf16[32,512]{1,0:T(8,128)(2,1)S(1)} collective-permute-done((bf16[32,512]{1,0:T(8,128)(2,1)S(1)}, bf16[32,512]{1,0:T(8,128)(2,1)S(1)}, u32[]{:S(2)}, u32[]{:S(2)}) %collective-permute-start.6) | collective-permute-done | bytes 32800 | tf_op jit(solution)/shard_map/ppermute | solution.py:33
  30.6 0.8 %collective-permute-done.7 = bf16[32,512]{1,0:T(8,128)(2,1)S(1)} collective-permute-done((bf16[32,512]{1,0:T(8,128)(2,1)S(1)}, bf16[32,512]{1,0:T(8,128)(2,1)S(1)}, u32[]{:S(2)}, u32[]{:S(2)}) %collective-permute-start.7) | collective-permute-done | bytes 32800 | tf_op jit(solution)/shard_map/ppermute | solution.py:33
  31.4 0.2 convolution_add_fusion.2
  31.6 0.0 collective-permute-done.8
  31.6 0.1 fusion.38
  31.8 0.1 collective-permute-start.9
  31.9 0.5 collective-permute-start.12
  32.4 0.7 %collective-permute-done.9 = f32[32,512]{1,0:T(8,128)S(1)} collective-permute-done((f32[32,512]{1,0:T(8,128)S(1)}, f32[32,512]{1,0:T(8,128)S(1)}, u32[]{:S(2)}, u32[]{:S(2)}) %collective-permute-start.9) | collective-permute-done | bytes 65568 | tf_op jit(solution)/shard_map/ppermute | solution.py:37
  33.1 2.8 %collective-permute-start.10 = (bf16[32,512]{1,0:T(8,128)(2,1)S(1)}, bf16[32,512]{1,0:T(8,128)(2,1)S(1)}, u32[]{:S(2)}, u32[]{:S(2)}) collective-permute-start(bf16[32,512]{1,0:T(8,128)(2,1)S(1)} %pad_maximum_fusion.8), channel_id=1, source_target_pairs={{12,0},{15,1},{14,2},{5,3},{2,4},{7,5},{4,6},{9,7},{6,8},{11,9},{8... | collective-permute-start | bytes 98312 | tf_op jit(solution)/shard_map/ppermute | solution.py:33
  35.9 0.0 collective-permute-start.11
  35.9 3.0 %collective-permute-done.10 = bf16[32,512]{1,0:T(8,128)(2,1)S(1)} collective-permute-done((bf16[32,512]{1,0:T(8,128)(2,1)S(1)}, bf16[32,512]{1,0:T(8,128)(2,1)S(1)}, u32[]{:S(2)}, u32[]{:S(2)}) %collective-permute-start.10) | collective-permute-done | bytes 32800 | tf_op jit(solution)/shard_map/ppermute | solution.py:33
  38.9 0.9 %collective-permute-done.11 = bf16[32,512]{1,0:T(8,128)(2,1)S(1)} collective-permute-done((bf16[32,512]{1,0:T(8,128)(2,1)S(1)}, bf16[32,512]{1,0:T(8,128)(2,1)S(1)}, u32[]{:S(2)}, u32[]{:S(2)}) %collective-permute-start.11) | collective-permute-done | bytes 32800 | tf_op jit(solution)/shard_map/ppermute | solution.py:33
  39.8 0.0 collective-permute-done.12
  39.8 0.1 fusion.42
  40.0 0.2 broadcast_select_fusion.1
  40.2 10.8 %all_to_all.10 = f32[16,4,256]{2,1,0:T(4,128)S(1)} all-to-all(f32[16,4,256]{2,1,0:T(4,128)S(1)} %bitcast.28), channel_id=1, replica_groups=mesh['groups'=2,'rows'=8,'cols'=2] {'rows','cols'}, dimensions={0} | all-to-all | bytes 131072 | tf_op jit(solution)/shard_map/all_to_all | solution.py:133
  51.1 0.6 %maximum_convert_fusion = bf16[8,4,256]{2,1,0:T(4,128)(2,1)} fusion(bf16[8,4,256]{2,1,0:T(4,128)(2,1)S(1)} %bitcast_reduce_fusion), kind=kLoop, calls=%fused_computation.68 | loop fusion | flops 24576 | bytes 32768 | tf_op jit(solution)/shard_map/convert_element_type | solution.py:135
  (24 shorter events, 0.2 us)
Async XLA Ops:
  0.0 11.5 %copy-start = (f32[4,1,1,256]{3,2,1,0:T(1,128)S(1)}, f32[4,1,1,256]{3,2,1,0:T(1,128)}, u32[]{:S(2)}) copy-start(f32[4,1,1,256]{3,2,1,0:T(1,128)} %param.7) | copy-start | bytes 12292
  1.4 14.3 %all-to-all-start = ((bf16[8,4,1280]{2,1,0:T(4,128)(2,1)}), bf16[8,4,1280]{2,1,0:T(4,128)(2,1)S(1)}, u32[]{:S(2)}, u32[]{:S(2)}) async-start(bf16[8,4,1280]{2,1,0:T(4,128)(2,1)} %shard_map.47), calls=%async_computation | async-start | bytes 163840 | tf_op jit(solution)/shard_map/all_to_all | solution.py:107
  11.5 4.4 %collective-permute-start = (bf16[256,256]{1,0:T(8,128)(2,1)S(1)}, bf16[256,256]{1,0:T(8,128)(2,1)S(1)}, u32[]{:S(2)}, u32[]{:S(2)}) collective-permute-start(bf16[256,256]{1,0:T(8,128)(2,1)S(1)} %get-tuple-element.20), channel_id=1, source_target_pairs={{0,1},{1,0},{2,3},{3,2},{4,5},{5,4},{6,7},{7,6},{8,9},{9,8},{10,11... | collective-permute-start | bytes 393224 | tf_op jit(solution)/shard_map/ppermute | solution.py:37
  16.1 1.3 %collective-permute-start.1 = (f32[32,512]{1,0:T(8,128)S(1)}, f32[32,512]{1,0:T(8,128)S(1)}, u32[]{:S(2)}, u32[]{:S(2)}) collective-permute-start(f32[32,512]{1,0:T(8,128)S(1)} %pad_maximum_fusion), channel_id=1, source_target_pairs={{0,1},{1,0},{2,3},{3,2},{4,5},{5,4},{6,7},{7,6},{8,9},{9,8},{10,11... | collective-permute-start | bytes 196616 | tf_op jit(solution)/shard_map/ppermute | solution.py:37
  16.1 7.3 %collective-permute-start.4 = (bf16[512,256]{1,0:T(8,128)(2,1)S(1)}, bf16[512,256]{1,0:T(8,128)(2,1)S(1)}, u32[]{:S(2)}, u32[]{:S(2)}) collective-permute-start(bf16[512,256]{1,0:T(8,128)(2,1)S(1)} %get-tuple-element.24), channel_id=1, source_target_pairs={{0,1},{1,0},{2,3},{3,2},{4,5},{5,4},{6,7},{7,6},{8,9},{9,8},{10,11... | collective-permute-start | bytes 786440 | tf_op jit(solution)/shard_map/ppermute | solution.py:37
  17.4 5.8 %collective-permute-start.2 = (bf16[32,512]{1,0:T(8,128)(2,1)S(1)}, bf16[32,512]{1,0:T(8,128)(2,1)S(1)}, u32[]{:S(2)}, u32[]{:S(2)}) collective-permute-start(bf16[32,512]{1,0:T(8,128)(2,1)S(1)} %pad_maximum_fusion.4), channel_id=1, source_target_pairs={{12,0},{15,1},{14,2},{5,3},{2,4},{7,5},{4,6},{9,7},{6,8},{11,9},{8... | collective-permute-start | bytes 98312 | tf_op jit(solution)/shard_map/ppermute | solution.py:33
  19.1 4.0 %collective-permute-start.3 = (bf16[32,512]{1,0:T(8,128)(2,1)S(1)}, bf16[32,512]{1,0:T(8,128)(2,1)S(1)}, u32[]{:S(2)}, u32[]{:S(2)}) collective-permute-start(bf16[32,512]{1,0:T(8,128)(2,1)S(1)} %pad_maximum_fusion.5), channel_id=1, source_target_pairs={{2,0},{5,1},{6,2},{1,3},{0,4},{9,5},{10,6},{3,7},{4,8},{13,9},{14,... | collective-permute-start | bytes 98312 | tf_op jit(solution)/shard_map/ppermute | solution.py:33
  23.5 1.3 %collective-permute-start.5 = (f32[32,512]{1,0:T(8,128)S(1)}, f32[32,512]{1,0:T(8,128)S(1)}, u32[]{:S(2)}, u32[]{:S(2)}) collective-permute-start(f32[32,512]{1,0:T(8,128)S(1)} %pad_maximum_fusion.1), channel_id=1, source_target_pairs={{0,1},{1,0},{2,3},{3,2},{4,5},{5,4},{6,7},{7,6},{8,9},{9,8},{10,11... | collective-permute-start | bytes 196616 | tf_op jit(solution)/shard_map/ppermute | solution.py:37
  23.8 7.8 %collective-permute-start.8 = (bf16[512,256]{1,0:T(8,128)(2,1)S(1)}, bf16[512,256]{1,0:T(8,128)(2,1)S(1)}, u32[]{:S(2)}, u32[]{:S(2)}) collective-permute-start(bf16[512,256]{1,0:T(8,128)(2,1)S(1)} %get-tuple-element.28), channel_id=1, source_target_pairs={{0,1},{1,0},{2,3},{3,2},{4,5},{5,4},{6,7},{7,6},{8,9},{9,8},{10,11... | collective-permute-start | bytes 786440 | tf_op jit(solution)/shard_map/ppermute | solution.py:37
  24.9 5.8 %collective-permute-start.6 = (bf16[32,512]{1,0:T(8,128)(2,1)S(1)}, bf16[32,512]{1,0:T(8,128)(2,1)S(1)}, u32[]{:S(2)}, u32[]{:S(2)}) collective-permute-start(bf16[32,512]{1,0:T(8,128)(2,1)S(1)} %pad_maximum_fusion.6), channel_id=1, source_target_pairs={{12,0},{15,1},{14,2},{5,3},{2,4},{7,5},{4,6},{9,7},{6,8},{11,9},{8... | collective-permute-start | bytes 98312 | tf_op jit(solution)/shard_map/ppermute | solution.py:33
  27.5 3.9 %collective-permute-start.7 = (bf16[32,512]{1,0:T(8,128)(2,1)S(1)}, bf16[32,512]{1,0:T(8,128)(2,1)S(1)}, u32[]{:S(2)}, u32[]{:S(2)}) collective-permute-start(bf16[32,512]{1,0:T(8,128)(2,1)S(1)} %pad_maximum_fusion.7), channel_id=1, source_target_pairs={{2,0},{5,1},{6,2},{1,3},{0,4},{9,5},{10,6},{3,7},{4,8},{13,9},{14,... | collective-permute-start | bytes 98312 | tf_op jit(solution)/shard_map/ppermute | solution.py:33
  31.8 1.3 %collective-permute-start.9 = (f32[32,512]{1,0:T(8,128)S(1)}, f32[32,512]{1,0:T(8,128)S(1)}, u32[]{:S(2)}, u32[]{:S(2)}) collective-permute-start(f32[32,512]{1,0:T(8,128)S(1)} %pad_maximum_fusion.2), channel_id=1, source_target_pairs={{0,1},{1,0},{2,3},{3,2},{4,5},{5,4},{6,7},{7,6},{8,9},{9,8},{10,11... | collective-permute-start | bytes 196616 | tf_op jit(solution)/shard_map/ppermute | solution.py:37
  31.9 8.0 %collective-permute-start.12 = (bf16[512,256]{1,0:T(8,128)(2,1)S(1)}, bf16[512,256]{1,0:T(8,128)(2,1)S(1)}, u32[]{:S(2)}, u32[]{:S(2)}) collective-permute-start(bf16[512,256]{1,0:T(8,128)(2,1)S(1)} %get-tuple-element.32), channel_id=1, source_target_pairs={{0,1},{1,0},{2,3},{3,2},{4,5},{5,4},{6,7},{7,6},{8,9},{9,8},{10,11... | collective-permute-start | bytes 786440 | tf_op jit(solution)/shard_map/ppermute | solution.py:37
  33.1 5.8 %collective-permute-start.10 = (bf16[32,512]{1,0:T(8,128)(2,1)S(1)}, bf16[32,512]{1,0:T(8,128)(2,1)S(1)}, u32[]{:S(2)}, u32[]{:S(2)}) collective-permute-start(bf16[32,512]{1,0:T(8,128)(2,1)S(1)} %pad_maximum_fusion.8), channel_id=1, source_target_pairs={{12,0},{15,1},{14,2},{5,3},{2,4},{7,5},{4,6},{9,7},{6,8},{11,9},{8... | collective-permute-start | bytes 98312 | tf_op jit(solution)/shard_map/ppermute | solution.py:33
  35.9 3.9 %collective-permute-start.11 = (bf16[32,512]{1,0:T(8,128)(2,1)S(1)}, bf16[32,512]{1,0:T(8,128)(2,1)S(1)}, u32[]{:S(2)}, u32[]{:S(2)}) collective-permute-start(bf16[32,512]{1,0:T(8,128)(2,1)S(1)} %pad_maximum_fusion.9), channel_id=1, source_target_pairs={{2,0},{5,1},{6,2},{1,3},{0,4},{9,5},{10,6},{3,7},{4,8},{13,9},{14,... | collective-permute-start | bytes 98312 | tf_op jit(solution)/shard_map/ppermute | solution.py:33

commit v4 on v3

--- a/solution.py
+++ b/solution.py
@@ -13,14 +13,15 @@
 
 
 def step_to(cycle, core, r, rows, where):
+    even = r % 2 == 0
+    first, last = r <= 1, r >= rows - 2
     if cycle == FAR:
-        before = where(r <= 1, -2, where(r == rows - 1, 1, -1))
-        after = where(r == 0, -1, where(r >= rows - 2, 2, 1))
+        on_core_0 = where(first, -2, where(last, 2, where(even, 1, -1)))
+        on_core_1 = where(even, -1, 1)
     else:
-        even = r % 2 == 0
-        before = where(even, where(r == 0, 1, -2), where(r == rows - 1, -1, 2))
-        after = where(even, where(r == rows - 2, 1, 2), where(r == 1, -1, -2))
-    return where(core == 0, before, after)
+        on_core_0 = where(first | last, where(even, 1, -1), where(r % 4 < 2, -2, 2))
+        on_core_1 = where(r % 4 < 2, 2, -2)
+    return where(core == 0, on_core_0, on_core_1)
 
 
 def from_source(value, cycle):

time: 52.1 us -> 50.3 us (0.965)
  waiting for transfers between devices: 18.2 us -> 16.9 us
  blocking collectives: 10.8 us -> 10.2 us
    ppermute x6, waiting for transfers between devices: 11.9 us -> 10.5 us  [from_source(): return lax.ppermute(value, ('rows', 'cols'), pairs)]
    all_to_all x1, blocking collectives: 10.8 us -> 10.2 us  [on_device(): lax.all_to_all(parts, ('rows', 'cols'), split_axis=0, concat_axis=0, tile...]
  transfers between devices with their start and end apart: 14 -> 14, of which waited for: 9 -> 8; matrix products, arithmetic and copies ran while one was open for 1% -> 1% of each run, Pallas kernels for 5% -> 6%
where the time goes in v4:
time: 50.3 us; the launch traced here: 49.9 us
  waiting for transfers between devices  16.9 us (34%)
  starting transfers between devices  16.3 us (32%)
  blocking collectives  10.2 us (20%)
  Pallas kernels  4.2 us (8%)
  matrix products  1.4 us (3%)
  other arithmetic  0.73 us (1%)
    ppermute x6, waiting for transfers between devices, from_source(): return lax.ppermute(value, ('rows', 'cols'), pairs)  10.5 us
    all_to_all x1, blocking collectives, on_device(): lax.all_to_all(parts, ('rows', 'cols'), split_axis=0, concat_axis=0, tile...  10.2 us
    ppermute x6, starting transfers between devices, from_source(): return lax.ppermute(value, ('rows', 'cols'), pairs)  7.28 us
    all_to_all x1, starting transfers between devices, on_device(): lax.all_to_all(expanded(features, rows, reach), 'rows', split_axis=0, con...  7.25 us
    all_to_all x1, waiting for transfers between devices, on_device(): lax.all_to_all(expanded(features, rows, reach), 'rows', split_axis=0, con...  4.08 us
    pallas_call x1, Pallas kernels, kept_weights(): pl.pallas_call(functools.partial(weight_kernel, plan, rows), out_shape=[p...  2.82 us
    ppermute x7, waiting for transfers between devices, partner(): lax.ppermute(value, 'cols', [(i, i ^ 1) for i in range(lax.axis_size('col...  2.24 us
    ppermute x7, starting transfers between devices, partner(): lax.ppermute(value, 'cols', [(i, i ^ 1) for i in range(lax.axis_size('col...  1.73 us
  transfers between devices with their start and end apart: 14, of which 8 were waited for; matrix products, arithmetic and copies ran while one was open for 1% of the time, Pallas kernels for 6%

profile of v4, /device:TPU:0, one launch (start us, length us, event | category | flops | bytes accessed | tf_op | source)
XLA Modules:
  0.0 49.9 jit_solution(9931192008751064687)
XLA Ops:
  0.0 0.0 copy-start
  0.0 1.4 %shard_map.47 = bf16[8,4,1280]{2,1,0:T(4,128)(2,1)} custom-call(bf16[4,2048]{1,0:T(4,128)(2,1)} %x_ref.1), custom_call_target="tpu_custom_call" | custom-call | tf_op jit(solution)/shard_map/pallas_call | solution.py:52
  1.4 7.3 %all-to-all-start = ((bf16[8,4,1280]{2,1,0:T(4,128)(2,1)}), bf16[8,4,1280]{2,1,0:T(4,128)(2,1)S(1)}, u32[]{:S(2)}, u32[]{:S(2)}) async-start(bf16[8,4,1280]{2,1,0:T(4,128)(2,1)} %shard_map.47), calls=%async_computation | async-start | bytes 163840 | tf_op jit(solution)/shard_map/all_to_all | solution.py:108
  8.6 2.8 %shard_map.46 = (bf16[1280,256]{1,0:T(8,128)(2,1)S(1)}, bf16[256,256]{1,0:T(8,128)(2,1)S(1)}, bf16[512,256]{1,0:T(8,128)(2,1)S(1)}, bf16[1024,256]{1,0:T(8,128)(...) custom-call(s32[4,6]{1,0:T(4,128)} %bitcast.35, ...), custom_call_target="tpu_custom_call" | custom-call | bytes 6291456 | tf_op jit(solution)/shard_map/pallas_call | solution.py:91
  11.5 0.1 collective-permute-start
  11.5 0.0 copy-done
  11.6 4.1 %all-to-all-done = bf16[8,4,1280]{2,1,0:T(4,128)(2,1)S(1)} async-done(((bf16[8,4,1280]{2,1,0:T(4,128)(2,1)}), bf16[8,4,1280]{2,1,0:T(4,128)(2,1)S(1)}, u32[]{:S(2)}, u32[]{:S(2)}) %all-to-all-start) | async-done | bytes 81952 | tf_op jit(solution)/shard_map/all_to_all | solution.py:108
  15.7 0.2 fusion
  15.9 0.0 collective-permute-done
  15.9 0.2 convolution_bitcast_fusion
  16.1 0.0 collective-permute-start.1
  16.1 0.5 collective-permute-start.4
  16.6 0.7 %collective-permute-done.1 = f32[32,512]{1,0:T(8,128)S(1)} collective-permute-done((f32[32,512]{1,0:T(8,128)S(1)}, f32[32,512]{1,0:T(8,128)S(1)}, u32[]{:S(2)}, u32[]{:S(2)}) %collective-permute-start.1) | collective-permute-done | bytes 65568 | tf_op jit(solution)/shard_map/ppermute | solution.py:38
  17.4 0.8 %collective-permute-start.2 = (bf16[32,512]{1,0:T(8,128)(2,1)S(1)}, bf16[32,512]{1,0:T(8,128)(2,1)S(1)}, u32[]{:S(2)}, u32[]{:S(2)}) collective-permute-start(bf16[32,512]{1,0:T(8,128)(2,1)S(1)} %pad_maximum_fusion.4), channel_id=1, source_target_pairs={{12,0},{15,1},{14,2},{5,3},{6,4},{3,5},{4,6},{9,7},{10,8},{7,9},{8... | collective-permute-start | bytes 98312 | tf_op jit(solution)/shard_map/ppermute | solution.py:34
  18.2 1.5 %collective-permute-start.3 = (bf16[32,512]{1,0:T(8,128)(2,1)S(1)}, bf16[32,512]{1,0:T(8,128)(2,1)S(1)}, u32[]{:S(2)}, u32[]{:S(2)}) collective-permute-start(bf16[32,512]{1,0:T(8,128)(2,1)S(1)} %pad_maximum_fusion.5), channel_id=1, source_target_pairs={{2,0},{5,1},{0,2},{7,3},{8,4},{1,5},{10,6},{3,7},{4,8},{13,9},{6,1... | collective-permute-start | bytes 98312 | tf_op jit(solution)/shard_map/ppermute | solution.py:34
  19.7 3.5 %collective-permute-done.2 = bf16[32,512]{1,0:T(8,128)(2,1)S(1)} collective-permute-done((bf16[32,512]{1,0:T(8,128)(2,1)S(1)}, bf16[32,512]{1,0:T(8,128)(2,1)S(1)}, u32[]{:S(2)}, u32[]{:S(2)}) %collective-permute-start.2) | collective-permute-done | bytes 32800 | tf_op jit(solution)/shard_map/ppermute | solution.py:34
  23.1 0.0 collective-permute-done.3
  23.2 0.2 convolution_add_fusion.3
  23.4 0.0 collective-permute-done.4
  23.4 0.1 fusion.34
  23.5 0.1 collective-permute-start.5
  23.6 0.5 collective-permute-start.8
  24.1 0.7 %collective-permute-done.5 = f32[32,512]{1,0:T(8,128)S(1)} collective-permute-done((f32[32,512]{1,0:T(8,128)S(1)}, f32[32,512]{1,0:T(8,128)S(1)}, u32[]{:S(2)}, u32[]{:S(2)}) %collective-permute-start.5) | collective-permute-done | bytes 65568 | tf_op jit(solution)/shard_map/ppermute | solution.py:38
  24.9 2.1 %collective-permute-start.6 = (bf16[32,512]{1,0:T(8,128)(2,1)S(1)}, bf16[32,512]{1,0:T(8,128)(2,1)S(1)}, u32[]{:S(2)}, u32[]{:S(2)}) collective-permute-start(bf16[32,512]{1,0:T(8,128)(2,1)S(1)} %pad_maximum_fusion.6), channel_id=1, source_target_pairs={{12,0},{15,1},{14,2},{5,3},{6,4},{3,5},{4,6},{9,7},{10,8},{7,9},{8... | collective-permute-start | bytes 98312 | tf_op jit(solution)/shard_map/ppermute | solution.py:34
  27.0 0.6 %collective-permute-start.7 = (bf16[32,512]{1,0:T(8,128)(2,1)S(1)}, bf16[32,512]{1,0:T(8,128)(2,1)S(1)}, u32[]{:S(2)}, u32[]{:S(2)}) collective-permute-start(bf16[32,512]{1,0:T(8,128)(2,1)S(1)} %pad_maximum_fusion.7), channel_id=1, source_target_pairs={{2,0},{5,1},{0,2},{7,3},{8,4},{1,5},{10,6},{3,7},{4,8},{13,9},{6,1... | collective-permute-start | bytes 98312 | tf_op jit(solution)/shard_map/ppermute | solution.py:34
  27.6 3.1 %collective-permute-done.6 = bf16[32,512]{1,0:T(8,128)(2,1)S(1)} collective-permute-done((bf16[32,512]{1,0:T(8,128)(2,1)S(1)}, bf16[32,512]{1,0:T(8,128)(2,1)S(1)}, u32[]{:S(2)}, u32[]{:S(2)}) %collective-permute-start.6) | collective-permute-done | bytes 32800 | tf_op jit(solution)/shard_map/ppermute | solution.py:34
  30.7 0.5 %collective-permute-done.7 = bf16[32,512]{1,0:T(8,128)(2,1)S(1)} collective-permute-done((bf16[32,512]{1,0:T(8,128)(2,1)S(1)}, bf16[32,512]{1,0:T(8,128)(2,1)S(1)}, u32[]{:S(2)}, u32[]{:S(2)}) %collective-permute-start.7) | collective-permute-done | bytes 32800 | tf_op jit(solution)/shard_map/ppermute | solution.py:34
  31.2 0.2 convolution_add_fusion.2
  31.4 0.0 collective-permute-done.8
  31.4 0.1 fusion.38
  31.5 0.1 collective-permute-start.9
  31.6 0.5 collective-permute-start.12
  32.1 0.7 %collective-permute-done.9 = f32[32,512]{1,0:T(8,128)S(1)} collective-permute-done((f32[32,512]{1,0:T(8,128)S(1)}, f32[32,512]{1,0:T(8,128)S(1)}, u32[]{:S(2)}, u32[]{:S(2)}) %collective-permute-start.9) | collective-permute-done | bytes 65568 | tf_op jit(solution)/shard_map/ppermute | solution.py:38
  32.9 1.6 %collective-permute-start.10 = (bf16[32,512]{1,0:T(8,128)(2,1)S(1)}, bf16[32,512]{1,0:T(8,128)(2,1)S(1)}, u32[]{:S(2)}, u32[]{:S(2)}) collective-permute-start(bf16[32,512]{1,0:T(8,128)(2,1)S(1)} %pad_maximum_fusion.8), channel_id=1, source_target_pairs={{12,0},{15,1},{14,2},{5,3},{6,4},{3,5},{4,6},{9,7},{10,8},{7,9},{8... | collective-permute-start | bytes 98312 | tf_op jit(solution)/shard_map/ppermute | solution.py:34
  34.5 0.7 %collective-permute-start.11 = (bf16[32,512]{1,0:T(8,128)(2,1)S(1)}, bf16[32,512]{1,0:T(8,128)(2,1)S(1)}, u32[]{:S(2)}, u32[]{:S(2)}) collective-permute-start(bf16[32,512]{1,0:T(8,128)(2,1)S(1)} %pad_maximum_fusion.9), channel_id=1, source_target_pairs={{2,0},{5,1},{0,2},{7,3},{8,4},{1,5},{10,6},{3,7},{4,8},{13,9},{6,1... | collective-permute-start | bytes 98312 | tf_op jit(solution)/shard_map/ppermute | solution.py:34
  35.2 3.5 %collective-permute-done.10 = bf16[32,512]{1,0:T(8,128)(2,1)S(1)} collective-permute-done((bf16[32,512]{1,0:T(8,128)(2,1)S(1)}, bf16[32,512]{1,0:T(8,128)(2,1)S(1)}, u32[]{:S(2)}, u32[]{:S(2)}) %collective-permute-start.10) | collective-permute-done | bytes 32800 | tf_op jit(solution)/shard_map/ppermute | solution.py:34
  38.7 0.0 collective-permute-done.11
  38.7 0.0 collective-permute-done.12
  38.7 0.1 fusion.42
  38.8 0.2 broadcast_select_fusion.1
  39.1 10.2 %all_to_all.10 = f32[16,4,256]{2,1,0:T(4,128)S(1)} all-to-all(f32[16,4,256]{2,1,0:T(4,128)S(1)} %bitcast.28), channel_id=1, replica_groups=mesh['groups'=2,'rows'=8,'cols'=2] {'rows','cols'}, dimensions={0} | all-to-all | bytes 131072 | tf_op jit(solution)/shard_map/all_to_all | solution.py:134
  49.3 0.6 %maximum_convert_fusion = bf16[8,4,256]{2,1,0:T(4,128)(2,1)} fusion(bf16[8,4,256]{2,1,0:T(4,128)(2,1)S(1)} %bitcast_reduce_fusion), kind=kLoop, calls=%fused_computation.68 | loop fusion | flops 24576 | bytes 32768 | tf_op jit(solution)/shard_map/convert_element_type | solution.py:136
  (24 shorter events, 0.2 us)
Async XLA Ops:
  0.0 11.5 %copy-start = (f32[4,1,1,256]{3,2,1,0:T(1,128)S(1)}, f32[4,1,1,256]{3,2,1,0:T(1,128)}, u32[]{:S(2)}) copy-start(f32[4,1,1,256]{3,2,1,0:T(1,128)} %param.7) | copy-start | bytes 12292
  1.4 14.3 %all-to-all-start = ((bf16[8,4,1280]{2,1,0:T(4,128)(2,1)}), bf16[8,4,1280]{2,1,0:T(4,128)(2,1)S(1)}, u32[]{:S(2)}, u32[]{:S(2)}) async-start(bf16[8,4,1280]{2,1,0:T(4,128)(2,1)} %shard_map.47), calls=%async_computation | async-start | bytes 163840 | tf_op jit(solution)/shard_map/all_to_all | solution.py:108
  11.5 4.4 %collective-permute-start = (bf16[256,256]{1,0:T(8,128)(2,1)S(1)}, bf16[256,256]{1,0:T(8,128)(2,1)S(1)}, u32[]{:S(2)}, u32[]{:S(2)}) collective-permute-start(bf16[256,256]{1,0:T(8,128)(2,1)S(1)} %get-tuple-element.20), channel_id=1, source_target_pairs={{0,1},{1,0},{2,3},{3,2},{4,5},{5,4},{6,7},{7,6},{8,9},{9,8},{10,11... | collective-permute-start | bytes 393224 | tf_op jit(solution)/shard_map/ppermute | solution.py:38
  16.1 1.3 %collective-permute-start.1 = (f32[32,512]{1,0:T(8,128)S(1)}, f32[32,512]{1,0:T(8,128)S(1)}, u32[]{:S(2)}, u32[]{:S(2)}) collective-permute-start(f32[32,512]{1,0:T(8,128)S(1)} %pad_maximum_fusion), channel_id=1, source_target_pairs={{0,1},{1,0},{2,3},{3,2},{4,5},{5,4},{6,7},{7,6},{8,9},{9,8},{10,11... | collective-permute-start | bytes 196616 | tf_op jit(solution)/shard_map/ppermute | solution.py:38
  16.1 7.3 %collective-permute-start.4 = (bf16[512,256]{1,0:T(8,128)(2,1)S(1)}, bf16[512,256]{1,0:T(8,128)(2,1)S(1)}, u32[]{:S(2)}, u32[]{:S(2)}) collective-permute-start(bf16[512,256]{1,0:T(8,128)(2,1)S(1)} %get-tuple-element.24), channel_id=1, source_target_pairs={{0,1},{1,0},{2,3},{3,2},{4,5},{5,4},{6,7},{7,6},{8,9},{9,8},{10,11... | collective-permute-start | bytes 786440 | tf_op jit(solution)/shard_map/ppermute | solution.py:38
  17.4 5.8 %collective-permute-start.2 = (bf16[32,512]{1,0:T(8,128)(2,1)S(1)}, bf16[32,512]{1,0:T(8,128)(2,1)S(1)}, u32[]{:S(2)}, u32[]{:S(2)}) collective-permute-start(bf16[32,512]{1,0:T(8,128)(2,1)S(1)} %pad_maximum_fusion.4), channel_id=1, source_target_pairs={{12,0},{15,1},{14,2},{5,3},{6,4},{3,5},{4,6},{9,7},{10,8},{7,9},{8... | collective-permute-start | bytes 98312 | tf_op jit(solution)/shard_map/ppermute | solution.py:34
  18.2 4.9 %collective-permute-start.3 = (bf16[32,512]{1,0:T(8,128)(2,1)S(1)}, bf16[32,512]{1,0:T(8,128)(2,1)S(1)}, u32[]{:S(2)}, u32[]{:S(2)}) collective-permute-start(bf16[32,512]{1,0:T(8,128)(2,1)S(1)} %pad_maximum_fusion.5), channel_id=1, source_target_pairs={{2,0},{5,1},{0,2},{7,3},{8,4},{1,5},{10,6},{3,7},{4,8},{13,9},{6,1... | collective-permute-start | bytes 98312 | tf_op jit(solution)/shard_map/ppermute | solution.py:34
  23.5 1.3 %collective-permute-start.5 = (f32[32,512]{1,0:T(8,128)S(1)}, f32[32,512]{1,0:T(8,128)S(1)}, u32[]{:S(2)}, u32[]{:S(2)}) collective-permute-start(f32[32,512]{1,0:T(8,128)S(1)} %pad_maximum_fusion.1), channel_id=1, source_target_pairs={{0,1},{1,0},{2,3},{3,2},{4,5},{5,4},{6,7},{7,6},{8,9},{9,8},{10,11... | collective-permute-start | bytes 196616 | tf_op jit(solution)/shard_map/ppermute | solution.py:38
  23.6 7.8 %collective-permute-start.8 = (bf16[512,256]{1,0:T(8,128)(2,1)S(1)}, bf16[512,256]{1,0:T(8,128)(2,1)S(1)}, u32[]{:S(2)}, u32[]{:S(2)}) collective-permute-start(bf16[512,256]{1,0:T(8,128)(2,1)S(1)} %get-tuple-element.28), channel_id=1, source_target_pairs={{0,1},{1,0},{2,3},{3,2},{4,5},{5,4},{6,7},{7,6},{8,9},{9,8},{10,11... | collective-permute-start | bytes 786440 | tf_op jit(solution)/shard_map/ppermute | solution.py:38
  24.9 5.8 %collective-permute-start.6 = (bf16[32,512]{1,0:T(8,128)(2,1)S(1)}, bf16[32,512]{1,0:T(8,128)(2,1)S(1)}, u32[]{:S(2)}, u32[]{:S(2)}) collective-permute-start(bf16[32,512]{1,0:T(8,128)(2,1)S(1)} %pad_maximum_fusion.6), channel_id=1, source_target_pairs={{12,0},{15,1},{14,2},{5,3},{6,4},{3,5},{4,6},{9,7},{10,8},{7,9},{8... | collective-permute-start | bytes 98312 | tf_op jit(solution)/shard_map/ppermute | solution.py:34
  27.0 4.2 %collective-permute-start.7 = (bf16[32,512]{1,0:T(8,128)(2,1)S(1)}, bf16[32,512]{1,0:T(8,128)(2,1)S(1)}, u32[]{:S(2)}, u32[]{:S(2)}) collective-permute-start(bf16[32,512]{1,0:T(8,128)(2,1)S(1)} %pad_maximum_fusion.7), channel_id=1, source_target_pairs={{2,0},{5,1},{0,2},{7,3},{8,4},{1,5},{10,6},{3,7},{4,8},{13,9},{6,1... | collective-permute-start | bytes 98312 | tf_op jit(solution)/shard_map/ppermute | solution.py:34
  31.5 1.3 %collective-permute-start.9 = (f32[32,512]{1,0:T(8,128)S(1)}, f32[32,512]{1,0:T(8,128)S(1)}, u32[]{:S(2)}, u32[]{:S(2)}) collective-permute-start(f32[32,512]{1,0:T(8,128)S(1)} %pad_maximum_fusion.2), channel_id=1, source_target_pairs={{0,1},{1,0},{2,3},{3,2},{4,5},{5,4},{6,7},{7,6},{8,9},{9,8},{10,11... | collective-permute-start | bytes 196616 | tf_op jit(solution)/shard_map/ppermute | solution.py:38
  31.6 7.1 %collective-permute-start.12 = (bf16[512,256]{1,0:T(8,128)(2,1)S(1)}, bf16[512,256]{1,0:T(8,128)(2,1)S(1)}, u32[]{:S(2)}, u32[]{:S(2)}) collective-permute-start(bf16[512,256]{1,0:T(8,128)(2,1)S(1)} %get-tuple-element.32), channel_id=1, source_target_pairs={{0,1},{1,0},{2,3},{3,2},{4,5},{5,4},{6,7},{7,6},{8,9},{9,8},{10,11... | collective-permute-start | bytes 786440 | tf_op jit(solution)/shard_map/ppermute | solution.py:38
  32.9 5.8 %collective-permute-start.10 = (bf16[32,512]{1,0:T(8,128)(2,1)S(1)}, bf16[32,512]{1,0:T(8,128)(2,1)S(1)}, u32[]{:S(2)}, u32[]{:S(2)}) collective-permute-start(bf16[32,512]{1,0:T(8,128)(2,1)S(1)} %pad_maximum_fusion.8), channel_id=1, source_target_pairs={{12,0},{15,1},{14,2},{5,3},{6,4},{3,5},{4,6},{9,7},{10,8},{7,9},{8... | collective-permute-start | bytes 98312 | tf_op jit(solution)/shard_map/ppermute | solution.py:34
  34.5 4.2 %collective-permute-start.11 = (bf16[32,512]{1,0:T(8,128)(2,1)S(1)}, bf16[32,512]{1,0:T(8,128)(2,1)S(1)}, u32[]{:S(2)}, u32[]{:S(2)}) collective-permute-start(bf16[32,512]{1,0:T(8,128)(2,1)S(1)} %pad_maximum_fusion.9), channel_id=1, source_target_pairs={{2,0},{5,1},{0,2},{7,3},{8,4},{1,5},{10,6},{3,7},{4,8},{13,9},{6,1... | collective-permute-start | bytes 98312 | tf_op jit(solution)/shard_map/ppermute | solution.py:34

commit v5 on v4

--- a/solution.py
+++ b/solution.py
@@ -38,12 +38,16 @@
     return lax.ppermute(value, "cols", [(i, i ^ 1) for i in range(lax.axis_size("cols"))])
 
 
+def in_turns(rows):
+    return [p // 2 if p % 2 == 0 else rows - 1 - p // 2 for p in range(rows)]
+
+
 def expand_kernel(reach, width, x_ref, o_ref):
     rows = o_ref.shape[0]
-    for r in range(rows):
+    for p, r in enumerate(in_turns(rows)):
         for m in range(2 * reach + 1):
             source = (r + m - reach) % rows
-            o_ref[r, :, m * width : (m + 1) * width] = x_ref[:, source * width : (source + 1) * width]
+            o_ref[p, :, m * width : (m + 1) * width] = x_ref[:, source * width : (source + 1) * width]
 
 
 def expanded(features, rows, reach):
@@ -105,7 +109,9 @@
     core = lax.axis_index("cols")
     samples = features.shape[0]
 
-    spread = lax.all_to_all(expanded(features, rows, reach), "rows", split_axis=0, concat_axis=0, tiled=True)
+    axes, turns = ("rows", "cols"), in_turns(rows)
+    halves = [[r * cols + c for r in turns] for c in range(cols)]
+    spread = lax.all_to_all(expanded(features, rows, reach), axes, 0, 0, axis_index_groups=halves, tiled=True)
     kept = kept_weights(weights[:, 0, 0], active[:, 0, 0], reach, rows)
     for_own = kept[0:1] + kept[3::2]
     for_other = [partner(w) for w in kept[1:2] + kept[2::2]]
@@ -131,9 +137,12 @@
     shape = (rows, samples, width)
     by_half = [jnp.where(core == h, part_own, part_other).reshape(shape) for h in range(cols)]
     parts = jnp.stack(by_half, axis=1).reshape(rows * cols, samples, width)
-    parts = lax.all_to_all(parts, ("rows", "cols"), split_axis=0, concat_axis=0, tiled=True)
+    everyone = [[r * cols + c for r in turns for c in range(cols)]]
+    parts = lax.all_to_all(parts, axes, 0, 0, axis_index_groups=everyone, tiled=True)
     total = parts.reshape(rows, cols, samples, width).sum(axis=1)
-    return jnp.maximum(total, 0.0).astype(jnp.bfloat16).transpose(1, 0, 2).reshape(samples, rows * width)
+    block = jnp.maximum(total, 0.0).astype(jnp.bfloat16)
+    block = jnp.concatenate([block[0::2], block[1::2][::-1]], axis=0)
+    return block.transpose(1, 0, 2).reshape(samples, rows * width)
 
 
 def solution(mesh):

time: 50.3 us -> 50.1 us (level)
  waiting for transfers between devices: 16.9 us -> 14.8 us
  starting transfers between devices: 16.3 us -> 18.3 us
    ppermute x6, starting transfers between devices: 7.28 us -> 9.31 us  [from_source(): return lax.ppermute(value, ('rows', 'cols'), pairs)]
    ppermute x6, waiting for transfers between devices: 10.5 us -> 8.88 us  [from_source(): return lax.ppermute(value, ('rows', 'cols'), pairs)]
    concatenate x0 -> x1, other arithmetic: none -> 0.62 us  [on_device(): block = jnp.concatenate([block[0::2], block[1::2][::-1]], axis=0)]
    convert_element_type x1, other arithmetic: 0.62 us -> 0.01 us  [on_device(): block = jnp.maximum(total, 0.0).astype(jnp.bfloat16)]
  transfers between devices with their start and end apart: 14 -> 14, of which waited for: 8 -> 9; matrix products, arithmetic and copies ran while one was open for 1% -> 1% of each run, Pallas kernels for 6% -> 6%
where the time goes in v5:
time: 50.1 us; the launch traced here: 49.7 us
  starting transfers between devices  18.3 us (37%)
  waiting for transfers between devices  14.8 us (30%)
  blocking collectives  9.99 us (20%)
  Pallas kernels  4.19 us (8%)
  matrix products  1.4 us (3%)
  other arithmetic  0.75 us (1%)
    all_to_all x1, blocking collectives, on_device(): lax.all_to_all(parts, axes, 0, 0, axis_index_groups=everyone, tiled=True)  9.99 us
    ppermute x6, starting transfers between devices, from_source(): return lax.ppermute(value, ('rows', 'cols'), pairs)  9.31 us
    ppermute x6, waiting for transfers between devices, from_source(): return lax.ppermute(value, ('rows', 'cols'), pairs)  8.88 us
    all_to_all x1, starting transfers between devices, on_device(): lax.all_to_all(expanded(features, rows, reach), axes, 0, 0, axis_index_gr...  7.25 us
    all_to_all x1, waiting for transfers between devices, on_device(): lax.all_to_all(expanded(features, rows, reach), axes, 0, 0, axis_index_gr...  3.64 us
    pallas_call x1, Pallas kernels, kept_weights(): pl.pallas_call(functools.partial(weight_kernel, plan, rows), out_shape=[p...  2.82 us
    ppermute x7, waiting for transfers between devices, partner(): lax.ppermute(value, 'cols', [(i, i ^ 1) for i in range(lax.axis_size('col...  2.24 us
    ppermute x7, starting transfers between devices, partner(): lax.ppermute(value, 'cols', [(i, i ^ 1) for i in range(lax.axis_size('col...  1.73 us
  transfers between devices with their start and end apart: 14, of which 9 were waited for; matrix products, arithmetic and copies ran while one was open for 1% of the time, Pallas kernels for 6%

profile of v5, /device:TPU:0, one launch (start us, length us, event | category | flops | bytes accessed | tf_op | source)
XLA Modules:
  0.0 49.7 jit_solution(13048330398137187767)
XLA Ops:
  0.0 0.0 copy-start
  0.0 1.4 %shard_map.47 = bf16[8,4,1280]{2,1,0:T(4,128)(2,1)} custom-call(bf16[4,2048]{1,0:T(4,128)(2,1)} %x_ref.1), custom_call_target="tpu_custom_call" | custom-call | tf_op jit(solution)/shard_map/pallas_call | solution.py:56
  1.4 7.3 %all-to-all-start = ((bf16[8,4,1280]{2,1,0:T(4,128)(2,1)}), bf16[8,4,1280]{2,1,0:T(4,128)(2,1)S(1)}, u32[]{:S(2)}, u32[]{:S(2)}) async-start(bf16[8,4,1280]{2,1,0:T(4,128)(2,1)} %shard_map.47), calls=%async_computation | async-start | bytes 163840 | tf_op jit(solution)/shard_map/all_to_all | solution.py:114
  8.6 2.8 %shard_map.46 = (bf16[1280,256]{1,0:T(8,128)(2,1)S(1)}, bf16[256,256]{1,0:T(8,128)(2,1)S(1)}, bf16[512,256]{1,0:T(8,128)(2,1)S(1)}, bf16[1024,256]{1,0:T(8,128)(...) custom-call(s32[4,6]{1,0:T(4,128)} %bitcast.35, ...), custom_call_target="tpu_custom_call" | custom-call | bytes 6291456 | tf_op jit(solution)/shard_map/pallas_call | solution.py:95
  11.5 0.1 collective-permute-start
  11.5 0.0 copy-done
  11.6 3.6 %all-to-all-done = bf16[8,4,1280]{2,1,0:T(4,128)(2,1)S(1)} async-done(((bf16[8,4,1280]{2,1,0:T(4,128)(2,1)}), bf16[8,4,1280]{2,1,0:T(4,128)(2,1)S(1)}, u32[]{:S(2)}, u32[]{:S(2)}) %all-to-all-start) | async-done | bytes 81952 | tf_op jit(solution)/shard_map/all_to_all | solution.py:114
  15.2 0.2 fusion
  15.4 0.0 collective-permute-done
  15.4 0.2 convolution_bitcast_fusion
  15.6 0.0 collective-permute-start.1
  15.7 0.5 collective-permute-start.4
  16.1 0.7 %collective-permute-done.1 = f32[32,512]{1,0:T(8,128)S(1)} collective-permute-done((f32[32,512]{1,0:T(8,128)S(1)}, f32[32,512]{1,0:T(8,128)S(1)}, u32[]{:S(2)}, u32[]{:S(2)}) %collective-permute-start.1) | collective-permute-done | bytes 65568 | tf_op jit(solution)/shard_map/ppermute | solution.py:38
  16.9 1.3 %collective-permute-start.2 = (bf16[32,512]{1,0:T(8,128)(2,1)S(1)}, bf16[32,512]{1,0:T(8,128)(2,1)S(1)}, u32[]{:S(2)}, u32[]{:S(2)}) collective-permute-start(bf16[32,512]{1,0:T(8,128)(2,1)S(1)} %pad_maximum_fusion.4), channel_id=1, source_target_pairs={{12,0},{15,1},{14,2},{5,3},{6,4},{3,5},{4,6},{9,7},{10,8},{7,9},{8... | collective-permute-start | bytes 98312 | tf_op jit(solution)/shard_map/ppermute | solution.py:34
  18.2 1.5 %collective-permute-start.3 = (bf16[32,512]{1,0:T(8,128)(2,1)S(1)}, bf16[32,512]{1,0:T(8,128)(2,1)S(1)}, u32[]{:S(2)}, u32[]{:S(2)}) collective-permute-start(bf16[32,512]{1,0:T(8,128)(2,1)S(1)} %pad_maximum_fusion.5), channel_id=1, source_target_pairs={{2,0},{5,1},{0,2},{7,3},{8,4},{1,5},{10,6},{3,7},{4,8},{13,9},{6,1... | collective-permute-start | bytes 98312 | tf_op jit(solution)/shard_map/ppermute | solution.py:34
  19.7 3.0 %collective-permute-done.2 = bf16[32,512]{1,0:T(8,128)(2,1)S(1)} collective-permute-done((bf16[32,512]{1,0:T(8,128)(2,1)S(1)}, bf16[32,512]{1,0:T(8,128)(2,1)S(1)}, u32[]{:S(2)}, u32[]{:S(2)}) %collective-permute-start.2) | collective-permute-done | bytes 32800 | tf_op jit(solution)/shard_map/ppermute | solution.py:34
  22.7 0.0 collective-permute-done.3
  22.7 0.2 convolution_add_fusion.3
  22.9 0.0 collective-permute-done.4
  22.9 0.1 fusion.34
  23.1 0.1 collective-permute-start.5
  23.2 0.5 collective-permute-start.8
  23.7 0.7 %collective-permute-done.5 = f32[32,512]{1,0:T(8,128)S(1)} collective-permute-done((f32[32,512]{1,0:T(8,128)S(1)}, f32[32,512]{1,0:T(8,128)S(1)}, u32[]{:S(2)}, u32[]{:S(2)}) %collective-permute-start.5) | collective-permute-done | bytes 65568 | tf_op jit(solution)/shard_map/ppermute | solution.py:38
  24.4 2.1 %collective-permute-start.6 = (bf16[32,512]{1,0:T(8,128)(2,1)S(1)}, bf16[32,512]{1,0:T(8,128)(2,1)S(1)}, u32[]{:S(2)}, u32[]{:S(2)}) collective-permute-start(bf16[32,512]{1,0:T(8,128)(2,1)S(1)} %pad_maximum_fusion.6), channel_id=1, source_target_pairs={{12,0},{15,1},{14,2},{5,3},{6,4},{3,5},{4,6},{9,7},{10,8},{7,9},{8... | collective-permute-start | bytes 98312 | tf_op jit(solution)/shard_map/ppermute | solution.py:34
  26.5 1.2 %collective-permute-start.7 = (bf16[32,512]{1,0:T(8,128)(2,1)S(1)}, bf16[32,512]{1,0:T(8,128)(2,1)S(1)}, u32[]{:S(2)}, u32[]{:S(2)}) collective-permute-start(bf16[32,512]{1,0:T(8,128)(2,1)S(1)} %pad_maximum_fusion.7), channel_id=1, source_target_pairs={{2,0},{5,1},{0,2},{7,3},{8,4},{1,5},{10,6},{3,7},{4,8},{13,9},{6,1... | collective-permute-start | bytes 98312 | tf_op jit(solution)/shard_map/ppermute | solution.py:34
  27.7 2.6 %collective-permute-done.6 = bf16[32,512]{1,0:T(8,128)(2,1)S(1)} collective-permute-done((bf16[32,512]{1,0:T(8,128)(2,1)S(1)}, bf16[32,512]{1,0:T(8,128)(2,1)S(1)}, u32[]{:S(2)}, u32[]{:S(2)}) %collective-permute-start.6) | collective-permute-done | bytes 32800 | tf_op jit(solution)/shard_map/ppermute | solution.py:34
  30.3 0.3 collective-permute-done.7
  30.7 0.2 convolution_add_fusion.2
  30.9 0.0 collective-permute-done.8
  30.9 0.1 fusion.38
  31.0 0.1 collective-permute-start.9
  31.1 0.5 collective-permute-start.12
  31.6 0.7 %collective-permute-done.9 = f32[32,512]{1,0:T(8,128)S(1)} collective-permute-done((f32[32,512]{1,0:T(8,128)S(1)}, f32[32,512]{1,0:T(8,128)S(1)}, u32[]{:S(2)}, u32[]{:S(2)}) %collective-permute-start.9) | collective-permute-done | bytes 65568 | tf_op jit(solution)/shard_map/ppermute | solution.py:38
  32.4 2.0 %collective-permute-start.10 = (bf16[32,512]{1,0:T(8,128)(2,1)S(1)}, bf16[32,512]{1,0:T(8,128)(2,1)S(1)}, u32[]{:S(2)}, u32[]{:S(2)}) collective-permute-start(bf16[32,512]{1,0:T(8,128)(2,1)S(1)} %pad_maximum_fusion.8), channel_id=1, source_target_pairs={{12,0},{15,1},{14,2},{5,3},{6,4},{3,5},{4,6},{9,7},{10,8},{7,9},{8... | collective-permute-start | bytes 98312 | tf_op jit(solution)/shard_map/ppermute | solution.py:34
  34.4 1.3 %collective-permute-start.11 = (bf16[32,512]{1,0:T(8,128)(2,1)S(1)}, bf16[32,512]{1,0:T(8,128)(2,1)S(1)}, u32[]{:S(2)}, u32[]{:S(2)}) collective-permute-start(bf16[32,512]{1,0:T(8,128)(2,1)S(1)} %pad_maximum_fusion.9), channel_id=1, source_target_pairs={{2,0},{5,1},{0,2},{7,3},{8,4},{1,5},{10,6},{3,7},{4,8},{13,9},{6,1... | collective-permute-start | bytes 98312 | tf_op jit(solution)/shard_map/ppermute | solution.py:34
  35.7 2.6 %collective-permute-done.10 = bf16[32,512]{1,0:T(8,128)(2,1)S(1)} collective-permute-done((bf16[32,512]{1,0:T(8,128)(2,1)S(1)}, bf16[32,512]{1,0:T(8,128)(2,1)S(1)}, u32[]{:S(2)}, u32[]{:S(2)}) %collective-permute-start.10) | collective-permute-done | bytes 32800 | tf_op jit(solution)/shard_map/ppermute | solution.py:34
  38.3 0.3 collective-permute-done.11
  38.6 0.0 collective-permute-done.12
  38.6 0.1 fusion.42
  38.7 0.2 broadcast_select_fusion.1
  39.0 10.0 %all_to_all.10 = f32[16,4,256]{2,1,0:T(4,128)S(1)} all-to-all(f32[16,4,256]{2,1,0:T(4,128)S(1)} %bitcast.28), channel_id=1, replica_groups={{0,1,14,15,2,3,12,13,4,5,10,11,6,7,8,9},{16,17,30,31,18,19,28,29,20,21,..., dimensions={0} | all-to-all | bytes 131072 | tf_op jit(solution)/shard_map/all_to_all | solution.py:141
  49.1 0.6 %pad_maximum_fusion.10 = bf16[8,4,256]{2,1,0:T(4,128)(2,1)} fusion(bf16[4,4,256]{2,1,0:T(4,128)(2,1)S(1)} %rev.3, bf16[4,4,256]{2,1,0:T(4,128)(2,1)S(1)} %get-tuple-element.53), kind=kLoop, calls=%fused_computation.70 | loop fusion | flops 8192 | bytes 32768 | tf_op jit(solution)/shard_map/concatenate | solution.py:144
  (27 shorter events, 0.2 us)
Async XLA Ops:
  0.0 11.5 %copy-start = (f32[4,1,1,256]{3,2,1,0:T(1,128)S(1)}, f32[4,1,1,256]{3,2,1,0:T(1,128)}, u32[]{:S(2)}) copy-start(f32[4,1,1,256]{3,2,1,0:T(1,128)} %param.7) | copy-start | bytes 12292
  1.4 13.8 %all-to-all-start = ((bf16[8,4,1280]{2,1,0:T(4,128)(2,1)}), bf16[8,4,1280]{2,1,0:T(4,128)(2,1)S(1)}, u32[]{:S(2)}, u32[]{:S(2)}) async-start(bf16[8,4,1280]{2,1,0:T(4,128)(2,1)} %shard_map.47), calls=%async_computation | async-start | bytes 163840 | tf_op jit(solution)/shard_map/all_to_all | solution.py:114
  11.5 4.0 %collective-permute-start = (bf16[256,256]{1,0:T(8,128)(2,1)S(1)}, bf16[256,256]{1,0:T(8,128)(2,1)S(1)}, u32[]{:S(2)}, u32[]{:S(2)}) collective-permute-start(bf16[256,256]{1,0:T(8,128)(2,1)S(1)} %get-tuple-element.20), channel_id=1, source_target_pairs={{0,1},{1,0},{2,3},{3,2},{4,5},{5,4},{6,7},{7,6},{8,9},{9,8},{10,11... | collective-permute-start | bytes 393224 | tf_op jit(solution)/shard_map/ppermute | solution.py:38
  15.6 1.3 %collective-permute-start.1 = (f32[32,512]{1,0:T(8,128)S(1)}, f32[32,512]{1,0:T(8,128)S(1)}, u32[]{:S(2)}, u32[]{:S(2)}) collective-permute-start(f32[32,512]{1,0:T(8,128)S(1)} %pad_maximum_fusion), channel_id=1, source_target_pairs={{0,1},{1,0},{2,3},{3,2},{4,5},{5,4},{6,7},{7,6},{8,9},{9,8},{10,11... | collective-permute-start | bytes 196616 | tf_op jit(solution)/shard_map/ppermute | solution.py:38
  15.7 7.3 %collective-permute-start.4 = (bf16[512,256]{1,0:T(8,128)(2,1)S(1)}, bf16[512,256]{1,0:T(8,128)(2,1)S(1)}, u32[]{:S(2)}, u32[]{:S(2)}) collective-permute-start(bf16[512,256]{1,0:T(8,128)(2,1)S(1)} %get-tuple-element.24), channel_id=1, source_target_pairs={{0,1},{1,0},{2,3},{3,2},{4,5},{5,4},{6,7},{7,6},{8,9},{9,8},{10,11... | collective-permute-start | bytes 786440 | tf_op jit(solution)/shard_map/ppermute | solution.py:38
  16.9 5.8 %collective-permute-start.2 = (bf16[32,512]{1,0:T(8,128)(2,1)S(1)}, bf16[32,512]{1,0:T(8,128)(2,1)S(1)}, u32[]{:S(2)}, u32[]{:S(2)}) collective-permute-start(bf16[32,512]{1,0:T(8,128)(2,1)S(1)} %pad_maximum_fusion.4), channel_id=1, source_target_pairs={{12,0},{15,1},{14,2},{5,3},{6,4},{3,5},{4,6},{9,7},{10,8},{7,9},{8... | collective-permute-start | bytes 98312 | tf_op jit(solution)/shard_map/ppermute | solution.py:34
  18.2 4.5 %collective-permute-start.3 = (bf16[32,512]{1,0:T(8,128)(2,1)S(1)}, bf16[32,512]{1,0:T(8,128)(2,1)S(1)}, u32[]{:S(2)}, u32[]{:S(2)}) collective-permute-start(bf16[32,512]{1,0:T(8,128)(2,1)S(1)} %pad_maximum_fusion.5), channel_id=1, source_target_pairs={{2,0},{5,1},{0,2},{7,3},{8,4},{1,5},{10,6},{3,7},{4,8},{13,9},{6,1... | collective-permute-start | bytes 98312 | tf_op jit(solution)/shard_map/ppermute | solution.py:34
  23.1 1.3 %collective-permute-start.5 = (f32[32,512]{1,0:T(8,128)S(1)}, f32[32,512]{1,0:T(8,128)S(1)}, u32[]{:S(2)}, u32[]{:S(2)}) collective-permute-start(f32[32,512]{1,0:T(8,128)S(1)} %pad_maximum_fusion.1), channel_id=1, source_target_pairs={{0,1},{1,0},{2,3},{3,2},{4,5},{5,4},{6,7},{7,6},{8,9},{9,8},{10,11... | collective-permute-start | bytes 196616 | tf_op jit(solution)/shard_map/ppermute | solution.py:38
  23.2 7.7 %collective-permute-start.8 = (bf16[512,256]{1,0:T(8,128)(2,1)S(1)}, bf16[512,256]{1,0:T(8,128)(2,1)S(1)}, u32[]{:S(2)}, u32[]{:S(2)}) collective-permute-start(bf16[512,256]{1,0:T(8,128)(2,1)S(1)} %get-tuple-element.28), channel_id=1, source_target_pairs={{0,1},{1,0},{2,3},{3,2},{4,5},{5,4},{6,7},{7,6},{8,9},{9,8},{10,11... | collective-permute-start | bytes 786440 | tf_op jit(solution)/shard_map/ppermute | solution.py:38
  24.4 5.9 %collective-permute-start.6 = (bf16[32,512]{1,0:T(8,128)(2,1)S(1)}, bf16[32,512]{1,0:T(8,128)(2,1)S(1)}, u32[]{:S(2)}, u32[]{:S(2)}) collective-permute-start(bf16[32,512]{1,0:T(8,128)(2,1)S(1)} %pad_maximum_fusion.6), channel_id=1, source_target_pairs={{12,0},{15,1},{14,2},{5,3},{6,4},{3,5},{4,6},{9,7},{10,8},{7,9},{8... | collective-permute-start | bytes 98312 | tf_op jit(solution)/shard_map/ppermute | solution.py:34
  26.5 4.1 %collective-permute-start.7 = (bf16[32,512]{1,0:T(8,128)(2,1)S(1)}, bf16[32,512]{1,0:T(8,128)(2,1)S(1)}, u32[]{:S(2)}, u32[]{:S(2)}) collective-permute-start(bf16[32,512]{1,0:T(8,128)(2,1)S(1)} %pad_maximum_fusion.7), channel_id=1, source_target_pairs={{2,0},{5,1},{0,2},{7,3},{8,4},{1,5},{10,6},{3,7},{4,8},{13,9},{6,1... | collective-permute-start | bytes 98312 | tf_op jit(solution)/shard_map/ppermute | solution.py:34
  31.0 1.3 %collective-permute-start.9 = (f32[32,512]{1,0:T(8,128)S(1)}, f32[32,512]{1,0:T(8,128)S(1)}, u32[]{:S(2)}, u32[]{:S(2)}) collective-permute-start(f32[32,512]{1,0:T(8,128)S(1)} %pad_maximum_fusion.2), channel_id=1, source_target_pairs={{0,1},{1,0},{2,3},{3,2},{4,5},{5,4},{6,7},{7,6},{8,9},{9,8},{10,11... | collective-permute-start | bytes 196616 | tf_op jit(solution)/shard_map/ppermute | solution.py:38
  31.1 7.5 %collective-permute-start.12 = (bf16[512,256]{1,0:T(8,128)(2,1)S(1)}, bf16[512,256]{1,0:T(8,128)(2,1)S(1)}, u32[]{:S(2)}, u32[]{:S(2)}) collective-permute-start(bf16[512,256]{1,0:T(8,128)(2,1)S(1)} %get-tuple-element.32), channel_id=1, source_target_pairs={{0,1},{1,0},{2,3},{3,2},{4,5},{5,4},{6,7},{7,6},{8,9},{9,8},{10,11... | collective-permute-start | bytes 786440 | tf_op jit(solution)/shard_map/ppermute | solution.py:38
  32.4 5.9 %collective-permute-start.10 = (bf16[32,512]{1,0:T(8,128)(2,1)S(1)}, bf16[32,512]{1,0:T(8,128)(2,1)S(1)}, u32[]{:S(2)}, u32[]{:S(2)}) collective-permute-start(bf16[32,512]{1,0:T(8,128)(2,1)S(1)} %pad_maximum_fusion.8), channel_id=1, source_target_pairs={{12,0},{15,1},{14,2},{5,3},{6,4},{3,5},{4,6},{9,7},{10,8},{7,9},{8... | collective-permute-start | bytes 98312 | tf_op jit(solution)/shard_map/ppermute | solution.py:34
  34.4 4.2 %collective-permute-start.11 = (bf16[32,512]{1,0:T(8,128)(2,1)S(1)}, bf16[32,512]{1,0:T(8,128)(2,1)S(1)}, u32[]{:S(2)}, u32[]{:S(2)}) collective-permute-start(bf16[32,512]{1,0:T(8,128)(2,1)S(1)} %pad_maximum_fusion.9), channel_id=1, source_target_pairs={{2,0},{5,1},{0,2},{7,3},{8,4},{1,5},{10,6},{3,7},{4,8},{13,9},{6,1... | collective-permute-start | bytes 98312 | tf_op jit(solution)/shard_map/ppermute | solution.py:34

commit v6 on v5

--- a/solution.py
+++ b/solution.py
@@ -102,11 +102,40 @@
     )(active, weights)
 
 
+def layer_kernel(both_ref, far_ref, near_ref, own_w_ref, other_w_ref, bias_ref, o_ref):
+    width = bias_ref.shape[-1]
+    first, second = slice(0, width), slice(width, 2 * width)
+    dot = functools.partial(jnp.dot, preferred_element_type=jnp.float32)
+    own_parts = [both_ref[:, first], both_ref[:, second], far_ref[:, first], near_ref[:, first]]
+    own = bias_ref[...]
+    for k, part in enumerate(own_parts):
+        own = own + dot(part, own_w_ref[k * width : (k + 1) * width, :])
+    other = dot(far_ref[:, second], other_w_ref[first, :]) + dot(near_ref[:, second], other_w_ref[second, :])
+    if len(o_ref.shape) == 2:
+        o_ref[:, first], o_ref[:, second] = own, other
+    else:
+        core, samples = lax.axis_index("cols"), o_ref.shape[2]
+        for p in range(o_ref.shape[0]):
+            o_ref[p, core] = own[p * samples : (p + 1) * samples]
+            o_ref[p, 1 - core] = other[p * samples : (p + 1) * samples]
+
+
+def partial_sums(both, far, near, own_w, other_w, bias, shape):
+    vmem = pl.BlockSpec(memory_space=pltpu.VMEM)
+    flops = 2 * both.shape[0] * (own_w.size + other_w.size)
+    return pl.pallas_call(
+        layer_kernel,
+        out_shape=pltpu.VMEM(shape, jnp.float32),
+        in_specs=[vmem] * 6,
+        out_specs=vmem,
+        cost_estimate=pl.CostEstimate(flops=flops, bytes_accessed=2 * own_w.size, transcendentals=0),
+    )(*(pltpu.with_memory_space_constraint(x, pltpu.VMEM) for x in (both, far, near, own_w, other_w, bias)))
+
+
 def on_device(features, weights, active, layer_bias):
     layer_count, _, _, candidates, width, _ = weights.shape
     reach = (candidates - 2) // 2
     rows, cols = lax.axis_size("rows"), lax.axis_size("cols")
-    core = lax.axis_index("cols")
     samples = features.shape[0]
 
     axes, turns = ("rows", "cols"), in_turns(rows)
@@ -121,22 +150,21 @@
         if layer:
             both = jnp.concatenate([own, other], axis=1)
             again = lax.optimization_barrier(jnp.concatenate(lax.optimization_barrier([own, other]), axis=1))
-            arrived = [both, from_source(both, FAR), from_source(again, NEAR)]
-            own, other = [x[:, :width] for x in arrived], [x[:, width:] for x in arrived]
-            to_own = jnp.concatenate([own[0], other[0]] + own[1:], axis=1)
-            to_other = jnp.concatenate(other[1:], axis=1)
+            shape = both.shape if layer < layer_count - 1 else (rows, cols, samples, width)
+            far_blocks, near_blocks = from_source(again, FAR), from_source(both, NEAR)
+            bias = layer_bias[layer, 0]
+            parts = partial_sums(both, far_blocks, near_blocks, for_own[layer], for_other[layer], bias, shape)
         else:
-            to_own, to_other = spread, spread[:, reach * width : (reach + 1) * width]
-        part_own = jnp.dot(to_own, for_own[layer], preferred_element_type=jnp.float32)
-        part_own = part_own + layer_bias[layer, 0, 0][None, :]
-        part_other = jnp.dot(to_other, for_other[layer], preferred_element_type=jnp.float32)
+            part_own = jnp.dot(spread, for_own[layer], preferred_element_type=jnp.float32)
+            part_own = part_own + layer_bias[layer, 0, 0][None, :]
+            block = spread[:, reach * width : (reach + 1) * width]
+            part_other = jnp.dot(block, for_other[layer], preferred_element_type=jnp.float32)
+            parts = jnp.concatenate([part_own, part_other], axis=1)
         if layer < layer_count - 1:
-            far = partner(jnp.concatenate([part_own, part_other], axis=1))
-            own = jnp.maximum(part_own + far[:, width:], 0.0).astype(jnp.bfloat16)
-            other = jnp.maximum(part_other + far[:, :width], 0.0).astype(jnp.bfloat16)
-    shape = (rows, samples, width)
-    by_half = [jnp.where(core == h, part_own, part_other).reshape(shape) for h in range(cols)]
-    parts = jnp.stack(by_half, axis=1).reshape(rows * cols, samples, width)
+            far = partner(parts)
+            own = jnp.maximum(parts[:, :width] + far[:, width:], 0.0).astype(jnp.bfloat16)
+            other = jnp.maximum(parts[:, width:] + far[:, :width], 0.0).astype(jnp.bfloat16)
+    parts = parts.reshape(rows * cols, samples, width)
     everyone = [[r * cols + c for r in turns for c in range(cols)]]
     parts = lax.all_to_all(parts, axes, 0, 0, axis_index_groups=everyone, tiled=True)
     total = parts.reshape(rows, cols, samples, width).sum(axis=1)

time: 50.1 us -> 49.6 us (0.990)
  matrix products: 1.4 us -> 0.37 us
  Pallas kernels: 4.19 us -> 4.92 us
    dot_general x8 -> x2, matrix products: 1.4 us -> 0.37 us  [the longest x1 0.2 us: on_device(): jnp.dot(spread, for_own[layer], preferred_element_type=jnp.float32)]
    pallas_call x0 -> x3, Pallas kernels: none -> 0.72 us  [partial_sums(): pl.pallas_call(layer_kernel, out_shape=pltpu.VMEM(shape, jnp.float32), in...]
where the time goes in v6:
time: 49.6 us; the launch traced here: 49.2 us
  starting transfers between devices  18.2 us (37%)
  waiting for transfers between devices  14.7 us (30%)
  blocking collectives  10.1 us (20%)
  Pallas kernels  4.92 us (10%)
  other arithmetic  0.72 us (1%)
    all_to_all x1, blocking collectives, on_device(): lax.all_to_all(parts, axes, 0, 0, axis_index_groups=everyone, tiled=True)  10.1 us
    ppermute x6, starting transfers between devices, from_source(): return lax.ppermute(value, ('rows', 'cols'), pairs)  9.34 us
    ppermute x6, waiting for transfers between devices, from_source(): return lax.ppermute(value, ('rows', 'cols'), pairs)  8.85 us
    all_to_all x1, starting transfers between devices, on_device(): lax.all_to_all(expanded(features, rows, reach), axes, 0, 0, axis_index_gr...  7.25 us
    all_to_all x1, waiting for transfers between devices, on_device(): lax.all_to_all(expanded(features, rows, reach), axes, 0, 0, axis_index_gr...  3.63 us
    pallas_call x1, Pallas kernels, kept_weights(): pl.pallas_call(functools.partial(weight_kernel, plan, rows), out_shape=[p...  2.82 us
    ppermute x7, waiting for transfers between devices, partner(): lax.ppermute(value, 'cols', [(i, i ^ 1) for i in range(lax.axis_size('col...  2.24 us
    ppermute x7, starting transfers between devices, partner(): lax.ppermute(value, 'cols', [(i, i ^ 1) for i in range(lax.axis_size('col...  1.66 us
  transfers between devices with their start and end apart: 14, of which 9 were waited for; matrix products, arithmetic and copies ran while one was open for 1% of the time, Pallas kernels for 6%

profile of v6, /device:TPU:0, one launch (start us, length us, event | category | flops | bytes accessed | tf_op | source)
XLA Modules:
  0.0 49.2 jit_solution(3420634784327520358)
XLA Ops:
  0.0 0.0 copy-start.1
  0.0 1.4 %shard_map.47 = bf16[8,4,1280]{2,1,0:T(4,128)(2,1)} custom-call(bf16[4,2048]{1,0:T(4,128)(2,1)} %x_ref.1), custom_call_target="tpu_custom_call" | custom-call | tf_op jit(solution)/shard_map/pallas_call | solution.py:56
  1.4 7.3 %all-to-all-start = ((bf16[8,4,1280]{2,1,0:T(4,128)(2,1)}), bf16[8,4,1280]{2,1,0:T(4,128)(2,1)S(1)}, u32[]{:S(2)}, u32[]{:S(2)}) async-start(bf16[8,4,1280]{2,1,0:T(4,128)(2,1)} %shard_map.47), calls=%async_computation | async-start | bytes 163840 | tf_op jit(solution)/shard_map/all_to_all | solution.py:143
  8.6 2.8 %shard_map.46 = (bf16[1280,256]{1,0:T(8,128)(2,1)S(1)}, bf16[256,256]{1,0:T(8,128)(2,1)S(1)}, bf16[512,256]{1,0:T(8,128)(2,1)S(1)}, bf16[1024,256]{1,0:T(8,128)(...) custom-call(s32[4,6]{1,0:T(4,128)} %bitcast.25, ...), custom_call_target="tpu_custom_call" | custom-call | bytes 6291456 | tf_op jit(solution)/shard_map/pallas_call | solution.py:95
  11.5 0.0 copy-start
  11.5 0.1 collective-permute-start
  11.6 0.0 copy-done.1
  11.6 3.6 %all-to-all-done = bf16[8,4,1280]{2,1,0:T(4,128)(2,1)S(1)} async-done(((bf16[8,4,1280]{2,1,0:T(4,128)(2,1)}), bf16[8,4,1280]{2,1,0:T(4,128)(2,1)S(1)}, u32[]{:S(2)}, u32[]{:S(2)}) %all-to-all-start) | async-done | bytes 81952 | tf_op jit(solution)/shard_map/all_to_all | solution.py:143
  15.2 0.2 fusion
  15.4 0.0 collective-permute-done
  15.4 0.2 convolution_bitcast_fusion
  15.6 0.0 collective-permute-start.1
  15.7 0.0 copy-done
  15.7 0.5 collective-permute-start.4
  16.2 0.7 %collective-permute-done.1 = f32[32,512]{1,0:T(8,128)S(1)} collective-permute-done((f32[32,512]{1,0:T(8,128)S(1)}, f32[32,512]{1,0:T(8,128)S(1)}, u32[]{:S(2)}, u32[]{:S(2)}) %collective-permute-start.1) | collective-permute-done | bytes 65568 | tf_op jit(solution)/shard_map/ppermute | solution.py:38
  16.9 1.3 %collective-permute-start.2 = (bf16[32,512]{1,0:T(8,128)(2,1)S(1)}, bf16[32,512]{1,0:T(8,128)(2,1)S(1)}, u32[]{:S(2)}, u32[]{:S(2)}) collective-permute-start(bf16[32,512]{1,0:T(8,128)(2,1)S(1)} %pad_maximum_fusion.2), channel_id=1, source_target_pairs={{12,0},{15,1},{14,2},{5,3},{6,4},{3,5},{4,6},{9,7},{10,8},{7,9},{8... | collective-permute-start | bytes 98312 | tf_op jit(solution)/shard_map/ppermute | solution.py:34
  18.2 1.5 %collective-permute-start.3 = (bf16[32,512]{1,0:T(8,128)(2,1)S(1)}, bf16[32,512]{1,0:T(8,128)(2,1)S(1)}, u32[]{:S(2)}, u32[]{:S(2)}) collective-permute-start(bf16[32,512]{1,0:T(8,128)(2,1)S(1)} %pad_maximum_fusion.1.both_ref), channel_id=1, source_target_pairs={{2,0},{5,1},{0,2},{7,3},{8,4},{1,5},{10,6},{3,7},{4,8},{13,9},{6,1... | collective-permute-start | bytes 98312 | tf_op jit(solution)/shard_map/ppermute | solution.py:34
  19.7 3.0 %collective-permute-done.2.far_ref = bf16[32,512]{1,0:T(8,128)(2,1)S(1)} collective-permute-done((bf16[32,512]{1,0:T(8,128)(2,1)S(1)}, bf16[32,512]{1,0:T(8,128)(2,1)S(1)}, u32[]{:S(2)}, u32[]{:S(2)}) %collective-permute-start.2) | collective-permute-done | bytes 32800 | tf_op jit(solution)/shard_map/ppermute | solution.py:34
  22.7 0.0 collective-permute-done.3.near_ref
  22.7 0.0 collective-permute-done.4.other_w_ref
  22.7 0.2 shard_map.48
  22.9 0.0 collective-permute-start.5
  23.0 0.5 %collective-permute-start.8 = (bf16[512,256]{1,0:T(8,128)(2,1)}, bf16[512,256]{1,0:T(8,128)(2,1)S(1)}, u32[]{:S(2)}, u32[]{:S(2)}) collective-permute-start(bf16[512,256]{1,0:T(8,128)(2,1)} %copy-done), channel_id=1, source_target_pairs={{0,1},{1,0},{2,3},{3,2},{4,5},{5,4},{6,7},{7,6},{8,9},{9,8},{10,11... | collective-permute-start | bytes 786440 | tf_op jit(solution)/shard_map/ppermute | solution.py:38
  23.5 0.7 %collective-permute-done.5 = f32[32,512]{1,0:T(8,128)S(1)} collective-permute-done((f32[32,512]{1,0:T(8,128)S(1)}, f32[32,512]{1,0:T(8,128)S(1)}, u32[]{:S(2)}, u32[]{:S(2)}) %collective-permute-start.5) | collective-permute-done | bytes 65568 | tf_op jit(solution)/shard_map/ppermute | solution.py:38
  24.3 2.1 %collective-permute-start.6 = (bf16[32,512]{1,0:T(8,128)(2,1)S(1)}, bf16[32,512]{1,0:T(8,128)(2,1)S(1)}, u32[]{:S(2)}, u32[]{:S(2)}) collective-permute-start(bf16[32,512]{1,0:T(8,128)(2,1)S(1)} %pad_maximum_fusion.4), channel_id=1, source_target_pairs={{12,0},{15,1},{14,2},{5,3},{6,4},{3,5},{4,6},{9,7},{10,8},{7,9},{8... | collective-permute-start | bytes 98312 | tf_op jit(solution)/shard_map/ppermute | solution.py:34
  26.4 1.2 %collective-permute-start.7 = (bf16[32,512]{1,0:T(8,128)(2,1)S(1)}, bf16[32,512]{1,0:T(8,128)(2,1)S(1)}, u32[]{:S(2)}, u32[]{:S(2)}) collective-permute-start(bf16[32,512]{1,0:T(8,128)(2,1)S(1)} %pad_maximum_fusion.3.both_ref), channel_id=1, source_target_pairs={{2,0},{5,1},{0,2},{7,3},{8,4},{1,5},{10,6},{3,7},{4,8},{13,9},{6,1... | collective-permute-start | bytes 98312 | tf_op jit(solution)/shard_map/ppermute | solution.py:34
  27.6 0.0 collective-permute-done.8.other_w_ref
  27.6 2.6 %collective-permute-done.6.far_ref = bf16[32,512]{1,0:T(8,128)(2,1)S(1)} collective-permute-done((bf16[32,512]{1,0:T(8,128)(2,1)S(1)}, bf16[32,512]{1,0:T(8,128)(2,1)S(1)}, u32[]{:S(2)}, u32[]{:S(2)}) %collective-permute-start.6) | collective-permute-done | bytes 32800 | tf_op jit(solution)/shard_map/ppermute | solution.py:34
  30.1 0.3 collective-permute-done.7.near_ref
  30.5 0.2 shard_map.49
  30.7 0.0 collective-permute-start.9
  30.8 0.5 %collective-permute-start.12 = (bf16[512,256]{1,0:T(8,128)(2,1)S(1)}, bf16[512,256]{1,0:T(8,128)(2,1)S(1)}, u32[]{:S(2)}, u32[]{:S(2)}) collective-permute-start(bf16[512,256]{1,0:T(8,128)(2,1)S(1)} %get-tuple-element.32), channel_id=1, source_target_pairs={{0,1},{1,0},{2,3},{3,2},{4,5},{5,4},{6,7},{7,6},{8,9},{9,8},{10,11... | collective-permute-start | bytes 786440 | tf_op jit(solution)/shard_map/ppermute | solution.py:38
  31.3 0.7 %collective-permute-done.9 = f32[32,512]{1,0:T(8,128)S(1)} collective-permute-done((f32[32,512]{1,0:T(8,128)S(1)}, f32[32,512]{1,0:T(8,128)S(1)}, u32[]{:S(2)}, u32[]{:S(2)}) %collective-permute-start.9) | collective-permute-done | bytes 65568 | tf_op jit(solution)/shard_map/ppermute | solution.py:38
  32.0 2.0 %collective-permute-start.10 = (bf16[32,512]{1,0:T(8,128)(2,1)S(1)}, bf16[32,512]{1,0:T(8,128)(2,1)S(1)}, u32[]{:S(2)}, u32[]{:S(2)}) collective-permute-start(bf16[32,512]{1,0:T(8,128)(2,1)S(1)} %pad_maximum_fusion.6), channel_id=1, source_target_pairs={{12,0},{15,1},{14,2},{5,3},{6,4},{3,5},{4,6},{9,7},{10,8},{7,9},{8... | collective-permute-start | bytes 98312 | tf_op jit(solution)/shard_map/ppermute | solution.py:34
  34.0 1.3 %collective-permute-start.11 = (bf16[32,512]{1,0:T(8,128)(2,1)S(1)}, bf16[32,512]{1,0:T(8,128)(2,1)S(1)}, u32[]{:S(2)}, u32[]{:S(2)}) collective-permute-start(bf16[32,512]{1,0:T(8,128)(2,1)S(1)} %pad_maximum_fusion.5.both_ref), channel_id=1, source_target_pairs={{2,0},{5,1},{0,2},{7,3},{8,4},{1,5},{10,6},{3,7},{4,8},{13,9},{6,1... | collective-permute-start | bytes 98312 | tf_op jit(solution)/shard_map/ppermute | solution.py:34
  35.3 0.0 collective-permute-done.12.other_w_ref
  35.3 2.6 %collective-permute-done.10.far_ref = bf16[32,512]{1,0:T(8,128)(2,1)S(1)} collective-permute-done((bf16[32,512]{1,0:T(8,128)(2,1)S(1)}, bf16[32,512]{1,0:T(8,128)(2,1)S(1)}, u32[]{:S(2)}, u32[]{:S(2)}) %collective-permute-start.10) | collective-permute-done | bytes 32800 | tf_op jit(solution)/shard_map/ppermute | solution.py:34
  37.9 0.3 collective-permute-done.11.near_ref
  38.2 0.2 shard_map.50
  38.5 10.1 %all_to_all.10 = f32[16,4,256]{2,1,0:T(4,128)S(1)} all-to-all(f32[16,4,256]{2,1,0:T(4,128)S(1)} %bitcast.22), channel_id=1, replica_groups={{0,1,14,15,2,3,12,13,4,5,10,11,6,7,8,9},{16,17,30,31,18,19,28,29,20,21,..., dimensions={0} | all-to-all | bytes 131072 | tf_op jit(solution)/shard_map/all_to_all | solution.py:169
  48.6 0.6 %pad_maximum_fusion.7 = bf16[8,4,256]{2,1,0:T(4,128)(2,1)} fusion(bf16[4,4,256]{2,1,0:T(4,128)(2,1)S(1)} %rev.3, bf16[4,4,256]{2,1,0:T(4,128)(2,1)S(1)} %get-tuple-element.39), kind=kLoop, calls=%fused_computation.31 | loop fusion | flops 8192 | bytes 32768 | tf_op jit(solution)/shard_map/concatenate | solution.py:172
  (16 shorter events, 0.1 us)
Async XLA Ops:
  0.0 11.6 %copy-start.1 = (f32[4,1,1,256]{3,2,1,0:T(1,128)S(1)}, f32[4,1,1,256]{3,2,1,0:T(1,128)}, u32[]{:S(2)}) copy-start(f32[4,1,1,256]{3,2,1,0:T(1,128)} %param.7) | copy-start | bytes 12292
  1.4 13.8 %all-to-all-start = ((bf16[8,4,1280]{2,1,0:T(4,128)(2,1)}), bf16[8,4,1280]{2,1,0:T(4,128)(2,1)S(1)}, u32[]{:S(2)}, u32[]{:S(2)}) async-start(bf16[8,4,1280]{2,1,0:T(4,128)(2,1)} %shard_map.47), calls=%async_computation | async-start | bytes 163840 | tf_op jit(solution)/shard_map/all_to_all | solution.py:143
  11.5 4.2 %copy-start = (bf16[512,256]{1,0:T(8,128)(2,1)}, bf16[512,256]{1,0:T(8,128)(2,1)S(1)}, u32[]{:S(2)}) copy-start(bf16[512,256]{1,0:T(8,128)(2,1)S(1)} %get-tuple-element.28) | copy-start | bytes 786436
  11.5 4.0 %collective-permute-start = (bf16[256,256]{1,0:T(8,128)(2,1)S(1)}, bf16[256,256]{1,0:T(8,128)(2,1)S(1)}, u32[]{:S(2)}, u32[]{:S(2)}) collective-permute-start(bf16[256,256]{1,0:T(8,128)(2,1)S(1)} %get-tuple-element.20), channel_id=1, source_target_pairs={{0,1},{1,0},{2,3},{3,2},{4,5},{5,4},{6,7},{7,6},{8,9},{9,8},{10,11... | collective-permute-start | bytes 393224 | tf_op jit(solution)/shard_map/ppermute | solution.py:38
  15.6 1.3 %collective-permute-start.1 = (f32[32,512]{1,0:T(8,128)S(1)}, f32[32,512]{1,0:T(8,128)S(1)}, u32[]{:S(2)}, u32[]{:S(2)}) collective-permute-start(f32[32,512]{1,0:T(8,128)S(1)} %pad_maximum_fusion), channel_id=1, source_target_pairs={{0,1},{1,0},{2,3},{3,2},{4,5},{5,4},{6,7},{7,6},{8,9},{9,8},{10,11... | collective-permute-start | bytes 196616 | tf_op jit(solution)/shard_map/ppermute | solution.py:38
  15.7 7.0 %collective-permute-start.4 = (bf16[512,256]{1,0:T(8,128)(2,1)S(1)}, bf16[512,256]{1,0:T(8,128)(2,1)S(1)}, u32[]{:S(2)}, u32[]{:S(2)}) collective-permute-start(bf16[512,256]{1,0:T(8,128)(2,1)S(1)} %get-tuple-element.24), channel_id=1, source_target_pairs={{0,1},{1,0},{2,3},{3,2},{4,5},{5,4},{6,7},{7,6},{8,9},{9,8},{10,11... | collective-permute-start | bytes 786440 | tf_op jit(solution)/shard_map/ppermute | solution.py:38
  16.9 5.8 %collective-permute-start.2 = (bf16[32,512]{1,0:T(8,128)(2,1)S(1)}, bf16[32,512]{1,0:T(8,128)(2,1)S(1)}, u32[]{:S(2)}, u32[]{:S(2)}) collective-permute-start(bf16[32,512]{1,0:T(8,128)(2,1)S(1)} %pad_maximum_fusion.2), channel_id=1, source_target_pairs={{12,0},{15,1},{14,2},{5,3},{6,4},{3,5},{4,6},{9,7},{10,8},{7,9},{8... | collective-permute-start | bytes 98312 | tf_op jit(solution)/shard_map/ppermute | solution.py:34
  18.2 4.5 %collective-permute-start.3 = (bf16[32,512]{1,0:T(8,128)(2,1)S(1)}, bf16[32,512]{1,0:T(8,128)(2,1)S(1)}, u32[]{:S(2)}, u32[]{:S(2)}) collective-permute-start(bf16[32,512]{1,0:T(8,128)(2,1)S(1)} %pad_maximum_fusion.1.both_ref), channel_id=1, source_target_pairs={{2,0},{5,1},{0,2},{7,3},{8,4},{1,5},{10,6},{3,7},{4,8},{13,9},{6,1... | collective-permute-start | bytes 98312 | tf_op jit(solution)/shard_map/ppermute | solution.py:34
  22.9 1.3 %collective-permute-start.5 = (f32[32,512]{1,0:T(8,128)S(1)}, f32[32,512]{1,0:T(8,128)S(1)}, u32[]{:S(2)}, u32[]{:S(2)}) collective-permute-start(f32[32,512]{1,0:T(8,128)S(1)} %shard_map.48), channel_id=1, source_target_pairs={{0,1},{1,0},{2,3},{3,2},{4,5},{5,4},{6,7},{7,6},{8,9},{9,8},{10,11... | collective-permute-start | bytes 196616 | tf_op jit(solution)/shard_map/ppermute | solution.py:38
  23.0 4.6 %collective-permute-start.8 = (bf16[512,256]{1,0:T(8,128)(2,1)}, bf16[512,256]{1,0:T(8,128)(2,1)S(1)}, u32[]{:S(2)}, u32[]{:S(2)}) collective-permute-start(bf16[512,256]{1,0:T(8,128)(2,1)} %copy-done), channel_id=1, source_target_pairs={{0,1},{1,0},{2,3},{3,2},{4,5},{5,4},{6,7},{7,6},{8,9},{9,8},{10,11... | collective-permute-start | bytes 786440 | tf_op jit(solution)/shard_map/ppermute | solution.py:38
  24.3 5.9 %collective-permute-start.6 = (bf16[32,512]{1,0:T(8,128)(2,1)S(1)}, bf16[32,512]{1,0:T(8,128)(2,1)S(1)}, u32[]{:S(2)}, u32[]{:S(2)}) collective-permute-start(bf16[32,512]{1,0:T(8,128)(2,1)S(1)} %pad_maximum_fusion.4), channel_id=1, source_target_pairs={{12,0},{15,1},{14,2},{5,3},{6,4},{3,5},{4,6},{9,7},{10,8},{7,9},{8... | collective-permute-start | bytes 98312 | tf_op jit(solution)/shard_map/ppermute | solution.py:34
  26.4 4.1 %collective-permute-start.7 = (bf16[32,512]{1,0:T(8,128)(2,1)S(1)}, bf16[32,512]{1,0:T(8,128)(2,1)S(1)}, u32[]{:S(2)}, u32[]{:S(2)}) collective-permute-start(bf16[32,512]{1,0:T(8,128)(2,1)S(1)} %pad_maximum_fusion.3.both_ref), channel_id=1, source_target_pairs={{2,0},{5,1},{0,2},{7,3},{8,4},{1,5},{10,6},{3,7},{4,8},{13,9},{6,1... | collective-permute-start | bytes 98312 | tf_op jit(solution)/shard_map/ppermute | solution.py:34
  30.7 1.3 %collective-permute-start.9 = (f32[32,512]{1,0:T(8,128)S(1)}, f32[32,512]{1,0:T(8,128)S(1)}, u32[]{:S(2)}, u32[]{:S(2)}) collective-permute-start(f32[32,512]{1,0:T(8,128)S(1)} %shard_map.49), channel_id=1, source_target_pairs={{0,1},{1,0},{2,3},{3,2},{4,5},{5,4},{6,7},{7,6},{8,9},{9,8},{10,11... | collective-permute-start | bytes 196616 | tf_op jit(solution)/shard_map/ppermute | solution.py:38
  30.8 4.5 %collective-permute-start.12 = (bf16[512,256]{1,0:T(8,128)(2,1)S(1)}, bf16[512,256]{1,0:T(8,128)(2,1)S(1)}, u32[]{:S(2)}, u32[]{:S(2)}) collective-permute-start(bf16[512,256]{1,0:T(8,128)(2,1)S(1)} %get-tuple-element.32), channel_id=1, source_target_pairs={{0,1},{1,0},{2,3},{3,2},{4,5},{5,4},{6,7},{7,6},{8,9},{9,8},{10,11... | collective-permute-start | bytes 786440 | tf_op jit(solution)/shard_map/ppermute | solution.py:38
  32.0 5.9 %collective-permute-start.10 = (bf16[32,512]{1,0:T(8,128)(2,1)S(1)}, bf16[32,512]{1,0:T(8,128)(2,1)S(1)}, u32[]{:S(2)}, u32[]{:S(2)}) collective-permute-start(bf16[32,512]{1,0:T(8,128)(2,1)S(1)} %pad_maximum_fusion.6), channel_id=1, source_target_pairs={{12,0},{15,1},{14,2},{5,3},{6,4},{3,5},{4,6},{9,7},{10,8},{7,9},{8... | collective-permute-start | bytes 98312 | tf_op jit(solution)/shard_map/ppermute | solution.py:34
  34.0 4.2 %collective-permute-start.11 = (bf16[32,512]{1,0:T(8,128)(2,1)S(1)}, bf16[32,512]{1,0:T(8,128)(2,1)S(1)}, u32[]{:S(2)}, u32[]{:S(2)}) collective-permute-start(bf16[32,512]{1,0:T(8,128)(2,1)S(1)} %pad_maximum_fusion.5.both_ref), channel_id=1, source_target_pairs={{2,0},{5,1},{0,2},{7,3},{8,4},{1,5},{10,6},{3,7},{4,8},{13,9},{6,1... | collective-permute-start | bytes 98312 | tf_op jit(solution)/shard_map/ppermute | solution.py:34
